TPU v7x, 128 devices: a whole 4x4x4 slice. The times are simulated.
128 devices in a mesh: blk: 4 (over z), dom: 32 (over x, y, core).
Axes of the slice: x: 4, y: 4, z: 4, core: 2. Of those that a mesh axis runs over, the one named last changes fastest.
Arguments:
- tiles: bfloat16 [49152, 128, 128], P(('blk', 'dom')), may hold values from -0.109375 to 0.109375
- tile_rows: int32 [49152], P(('blk', 'dom')), may hold values from 0 to 511, as said below
- tile_cols: int32 [49152], P(('blk', 'dom')), may hold values from 0 to 511, as said below
- tile_counts: int32 [128], P(('blk', 'dom')), may hold values from 32 to 384, as said below
- loads_in: bfloat16 [65536, 512], P(('blk', 'dom')), may hold values from -6 to 6
Outputs:
- response: float32 [65536, 512], P(('blk', 'dom'))
Inputs may be any that keep to these rules, and one draw needn't show every extreme that they name: `tile_counts`: one device has exactly 384 live slots in every draw. `tile_rows`: for the device at index b of blk, every live slot names a block row in [b * 128, (b + 1) * 128); within a device the live slots' block rows never fall from one slot to the next. Slots at or past a device's count are ignored. `tile_cols`: for the device at index d of dom, every slot names a block column c such that c // 4 equals d modulo the number of devices along dom. (row, column) pairs may repeat; repeated tiles add.
All inputs are finite; a program needn't handle non-finite values.
Results may differ from a plain program's by a relative error of at most 0.0003.
Values may be sent and summed in bfloat16 or wider, within the bound.
No kernel may reach another device: no remote copies, remote signals or barrier semaphores. Data moves between devices by JAX's collectives and lax.ppermute only.
A program may use at most 192 MiB of HBM per device.

v0:
```python
import math

import jax
import jax.numpy as jnp
from jax import lax
from jax.sharding import PartitionSpec as P


def add_tiles(term, tiles, rows_here, xblocks, xindex, usable, last):
    slots = tiles.shape[0]
    group = math.gcd(slots, 32)
    nblk = term.shape[0]
    turns = (last + group - 1) // group

    def step(turn, acc):
        index = turn * group + jnp.arange(group, dtype=jnp.int32)
        safe = jnp.minimum(index, slots - 1)
        valid = (index < last) & jnp.take(usable, safe)
        tile_group = jnp.take(tiles, safe, axis=0)
        where_x = jnp.clip(jnp.take(xindex, safe), 0, xblocks.shape[0] - 1)
        xgroup = jnp.take(xblocks, where_x, axis=0)
        prods = jnp.einsum("gij,gjc->gic", tile_group, xgroup, preferred_element_type=jnp.float32)
        target = jnp.where(valid, jnp.take(rows_here, safe), nblk)
        return acc.at[target].add(prods, mode="drop")

    return lax.fori_loop(0, turns, step, term)


def shards(tiles, tile_rows, tile_cols, tile_counts, loads_in):
    blk = tiles.shape[1]
    loads = loads_in.shape[1]
    pb = loads_in.shape[0] // blk
    n_dom = lax.axis_size("dom")
    rgroup = pb * n_dom
    count = tile_counts[0]
    rows_local = tile_rows - lax.axis_index("blk") * rgroup
    xindex = tile_cols // pb // n_dom * pb + tile_cols % pb
    everyone = jnp.ones(tile_rows.shape, dtype=bool)
    empty = jnp.zeros((rgroup, blk, loads), jnp.float32)
    gathered = lax.all_gather(loads_in, "blk", axis=0, tiled=True)
    xblocks = gathered.reshape(gathered.shape[0] // blk, blk, loads)
    partial_value = add_tiles(empty, tiles, rows_local, xblocks, xindex, everyone, count)
    result = lax.psum_scatter(
        partial_value.reshape(rgroup * blk, loads), "dom", scatter_dimension=0, tiled=True
    )
    return result


def solution(mesh):
    in_specs = (
        P(("blk", "dom"), None, None),
        P(("blk", "dom")),
        P(("blk", "dom")),
        P(("blk", "dom")),
        P(("blk", "dom"), None),
    )
    out_specs = P(("blk", "dom"), None)
    return jax.shard_map(shards, mesh=mesh, in_specs=in_specs, out_specs=out_specs, check_vma=False)
```

profile of v0, /device:TPU:14, one launch (start us, length us, event | category | flops | bytes accessed | tf_op | source)
XLA Modules:
  0.0 644.7 jit_solution(2894285634227512714)
XLA Ops:
  8.7 33.6 %all-gather.2.cloned.1.call-done = bf16[2048,512]{1,0:T(8,128)(2,1)} async-done(((bf16[512,512]{1,0:T(8,128)(2,1)}), bf16[2048,512]{1,0:T(8,128)(2,1)}) %all-gather.2.cloned.1.call-update) | async-done | bytes 2097168 | tf_op jit(solution)/shard_map/all_gather | solution.py:40
  42.3 11.2 %broadcast_in_dim.47 = f32[128,128,512]{2,1,0:T(8,128)} broadcast(f32[]{:T(128)} %constant.117.clone.1), dimensions={} | broadcast | bytes 33554436 | tf_op jit(solution)/shard_map/broadcast_in_dim | solution.py:39
  53.6 419.0 %while.10 = (s32[]{:T(128)}, f32[128,128,512]{2,1,0:T(8,128)}, s32[]{:T(128)}, s32[]{:T(128)}, s32[384]{0:T(512)S(1)}, /*index=5*/bf16[384,128,128]{2,1,0:T(8,12...) while((s32[]{:T(128)}, f32[128,128,512]{2,1,0:T(8,128)}, ...), condition=%wide.region_2.4_spmd, body=%wide.region_0.3_spmd.sunk | while | flops 541593920 | bytes 49298540 | solution.py:26
  56.5 5.3 gather_fusion.4
  61.8 2.7 gather_fusion.3
  64.6 6.7 %fusion.21 = f32[32,128,512]{2,1,0:T(8,128)} fusion(bf16[32,128,512]{2,1,0:T(8,128)(2,1)} %gather_fusion.3, pred[32]{0:T(512)(128)(4,1)S(1)} %get-tuple-element.125, bf16[32,128,128]{2,1,0:T(8,128)(2,1)S(1)} %gather_fusion.4, pred[32]{0:T(512)(128)(4,1)S(1)} %get-tuple-element.126), kind=kOutput, calls=%fused_computation.6.clone.1 | convolution fusion | flops 539492352 | bytes 13631552 | tf_op jit(solution)/shard_map/while/body/gij,gjc->gic/dot_general | solution.py:22
  71.3 17.0 %scatter_fusion = f32[128,128,512]{2,1,0:T(8,128)} fusion(f32[128,128,512]{2,1,0:T(8,128)} %get-tuple-element.139, s32[32]{0:T(128)S(1)} %compare_select_fusion.8, f32[32,128,512]{2,1,0:T(8,128)} %fusion.21), kind=kCustom, calls=%fused_computation.5.clone.1 | custom fusion | flops 2097152 | bytes 25165952 | tf_op jit(solution)/shard_map/while/body/scatter-add | solution.py:24
  91.2 5.3 gather_fusion.4
  96.5 2.7 gather_fusion.3
  99.3 6.7 %fusion.21 = f32[32,128,512]{2,1,0:T(8,128)} fusion(bf16[32,128,512]{2,1,0:T(8,128)(2,1)} %gather_fusion.3, pred[32]{0:T(512)(128)(4,1)S(1)} %get-tuple-element.125, bf16[32,128,128]{2,1,0:T(8,128)(2,1)S(1)} %gather_fusion.4, pred[32]{0:T(512)(128)(4,1)S(1)} %get-tuple-element.126), kind=kOutput, calls=%fused_computation.6.clone.1 | convolution fusion | flops 539492352 | bytes 13631552 | tf_op jit(solution)/shard_map/while/body/gij,gjc->gic/dot_general | solution.py:22
  106.0 17.5 %scatter_fusion = f32[128,128,512]{2,1,0:T(8,128)} fusion(f32[128,128,512]{2,1,0:T(8,128)} %get-tuple-element.139, s32[32]{0:T(128)S(1)} %compare_select_fusion.8, f32[32,128,512]{2,1,0:T(8,128)} %fusion.21), kind=kCustom, calls=%fused_computation.5.clone.1 | custom fusion | flops 2097152 | bytes 25165952 | tf_op jit(solution)/shard_map/while/body/scatter-add | solution.py:24
  126.4 5.3 gather_fusion.4
  131.7 2.7 gather_fusion.3
  134.5 6.7 %fusion.21 = f32[32,128,512]{2,1,0:T(8,128)} fusion(bf16[32,128,512]{2,1,0:T(8,128)(2,1)} %gather_fusion.3, pred[32]{0:T(512)(128)(4,1)S(1)} %get-tuple-element.125, bf16[32,128,128]{2,1,0:T(8,128)(2,1)S(1)} %gather_fusion.4, pred[32]{0:T(512)(128)(4,1)S(1)} %get-tuple-element.126), kind=kOutput, calls=%fused_computation.6.clone.1 | convolution fusion | flops 539492352 | bytes 13631552 | tf_op jit(solution)/shard_map/while/body/gij,gjc->gic/dot_general | solution.py:22
  141.2 17.5 %scatter_fusion = f32[128,128,512]{2,1,0:T(8,128)} fusion(f32[128,128,512]{2,1,0:T(8,128)} %get-tuple-element.139, s32[32]{0:T(128)S(1)} %compare_select_fusion.8, f32[32,128,512]{2,1,0:T(8,128)} %fusion.21), kind=kCustom, calls=%fused_computation.5.clone.1 | custom fusion | flops 2097152 | bytes 25165952 | tf_op jit(solution)/shard_map/while/body/scatter-add | solution.py:24
  161.5 5.3 gather_fusion.4
  166.9 2.7 gather_fusion.3
  169.6 6.7 %fusion.21 = f32[32,128,512]{2,1,0:T(8,128)} fusion(bf16[32,128,512]{2,1,0:T(8,128)(2,1)} %gather_fusion.3, pred[32]{0:T(512)(128)(4,1)S(1)} %get-tuple-element.125, bf16[32,128,128]{2,1,0:T(8,128)(2,1)S(1)} %gather_fusion.4, pred[32]{0:T(512)(128)(4,1)S(1)} %get-tuple-element.126), kind=kOutput, calls=%fused_computation.6.clone.1 | convolution fusion | flops 539492352 | bytes 13631552 | tf_op jit(solution)/shard_map/while/body/gij,gjc->gic/dot_general | solution.py:22
  176.3 17.4 %scatter_fusion = f32[128,128,512]{2,1,0:T(8,128)} fusion(f32[128,128,512]{2,1,0:T(8,128)} %get-tuple-element.139, s32[32]{0:T(128)S(1)} %compare_select_fusion.8, f32[32,128,512]{2,1,0:T(8,128)} %fusion.21), kind=kCustom, calls=%fused_computation.5.clone.1 | custom fusion | flops 2097152 | bytes 25165952 | tf_op jit(solution)/shard_map/while/body/scatter-add | solution.py:24
  196.6 5.3 gather_fusion.4
  202.0 2.7 gather_fusion.3
  204.7 6.7 %fusion.21 = f32[32,128,512]{2,1,0:T(8,128)} fusion(bf16[32,128,512]{2,1,0:T(8,128)(2,1)} %gather_fusion.3, pred[32]{0:T(512)(128)(4,1)S(1)} %get-tuple-element.125, bf16[32,128,128]{2,1,0:T(8,128)(2,1)S(1)} %gather_fusion.4, pred[32]{0:T(512)(128)(4,1)S(1)} %get-tuple-element.126), kind=kOutput, calls=%fused_computation.6.clone.1 | convolution fusion | flops 539492352 | bytes 13631552 | tf_op jit(solution)/shard_map/while/body/gij,gjc->gic/dot_general | solution.py:22
  211.4 17.3 %scatter_fusion = f32[128,128,512]{2,1,0:T(8,128)} fusion(f32[128,128,512]{2,1,0:T(8,128)} %get-tuple-element.139, s32[32]{0:T(128)S(1)} %compare_select_fusion.8, f32[32,128,512]{2,1,0:T(8,128)} %fusion.21), kind=kCustom, calls=%fused_computation.5.clone.1 | custom fusion | flops 2097152 | bytes 25165952 | tf_op jit(solution)/shard_map/while/body/scatter-add | solution.py:24
  231.5 5.3 gather_fusion.4
  236.9 2.7 gather_fusion.3
  239.6 6.7 %fusion.21 = f32[32,128,512]{2,1,0:T(8,128)} fusion(bf16[32,128,512]{2,1,0:T(8,128)(2,1)} %gather_fusion.3, pred[32]{0:T(512)(128)(4,1)S(1)} %get-tuple-element.125, bf16[32,128,128]{2,1,0:T(8,128)(2,1)S(1)} %gather_fusion.4, pred[32]{0:T(512)(128)(4,1)S(1)} %get-tuple-element.126), kind=kOutput, calls=%fused_computation.6.clone.1 | convolution fusion | flops 539492352 | bytes 13631552 | tf_op jit(solution)/shard_map/while/body/gij,gjc->gic/dot_general | solution.py:22
  246.3 17.6 %scatter_fusion = f32[128,128,512]{2,1,0:T(8,128)} fusion(f32[128,128,512]{2,1,0:T(8,128)} %get-tuple-element.139, s32[32]{0:T(128)S(1)} %compare_select_fusion.8, f32[32,128,512]{2,1,0:T(8,128)} %fusion.21), kind=kCustom, calls=%fused_computation.5.clone.1 | custom fusion | flops 2097152 | bytes 25165952 | tf_op jit(solution)/shard_map/while/body/scatter-add | solution.py:24
  266.8 5.3 gather_fusion.4
  272.2 2.7 gather_fusion.3
  274.9 6.7 %fusion.21 = f32[32,128,512]{2,1,0:T(8,128)} fusion(bf16[32,128,512]{2,1,0:T(8,128)(2,1)} %gather_fusion.3, pred[32]{0:T(512)(128)(4,1)S(1)} %get-tuple-element.125, bf16[32,128,128]{2,1,0:T(8,128)(2,1)S(1)} %gather_fusion.4, pred[32]{0:T(512)(128)(4,1)S(1)} %get-tuple-element.126), kind=kOutput, calls=%fused_computation.6.clone.1 | convolution fusion | flops 539492352 | bytes 13631552 | tf_op jit(solution)/shard_map/while/body/gij,gjc->gic/dot_general | solution.py:22
  281.6 17.3 %scatter_fusion = f32[128,128,512]{2,1,0:T(8,128)} fusion(f32[128,128,512]{2,1,0:T(8,128)} %get-tuple-element.139, s32[32]{0:T(128)S(1)} %compare_select_fusion.8, f32[32,128,512]{2,1,0:T(8,128)} %fusion.21), kind=kCustom, calls=%fused_computation.5.clone.1 | custom fusion | flops 2097152 | bytes 25165952 | tf_op jit(solution)/shard_map/while/body/scatter-add | solution.py:24
  301.8 5.3 gather_fusion.4
  307.1 2.7 gather_fusion.3
  309.9 6.7 %fusion.21 = f32[32,128,512]{2,1,0:T(8,128)} fusion(bf16[32,128,512]{2,1,0:T(8,128)(2,1)} %gather_fusion.3, pred[32]{0:T(512)(128)(4,1)S(1)} %get-tuple-element.125, bf16[32,128,128]{2,1,0:T(8,128)(2,1)S(1)} %gather_fusion.4, pred[32]{0:T(512)(128)(4,1)S(1)} %get-tuple-element.126), kind=kOutput, calls=%fused_computation.6.clone.1 | convolution fusion | flops 539492352 | bytes 13631552 | tf_op jit(solution)/shard_map/while/body/gij,gjc->gic/dot_general | solution.py:22
  316.6 17.4 %scatter_fusion = f32[128,128,512]{2,1,0:T(8,128)} fusion(f32[128,128,512]{2,1,0:T(8,128)} %get-tuple-element.139, s32[32]{0:T(128)S(1)} %compare_select_fusion.8, f32[32,128,512]{2,1,0:T(8,128)} %fusion.21), kind=kCustom, calls=%fused_computation.5.clone.1 | custom fusion | flops 2097152 | bytes 25165952 | tf_op jit(solution)/shard_map/while/body/scatter-add | solution.py:24
  336.9 5.3 gather_fusion.4
  344.9 6.7 %fusion.21 = f32[32,128,512]{2,1,0:T(8,128)} fusion(bf16[32,128,512]{2,1,0:T(8,128)(2,1)} %gather_fusion.3, pred[32]{0:T(512)(128)(4,1)S(1)} %get-tuple-element.125, bf16[32,128,128]{2,1,0:T(8,128)(2,1)S(1)} %gather_fusion.4, pred[32]{0:T(512)(128)(4,1)S(1)} %get-tuple-element.126), kind=kOutput, calls=%fused_computation.6.clone.1 | convolution fusion | flops 539492352 | bytes 13631552 | tf_op jit(solution)/shard_map/while/body/gij,gjc->gic/dot_general | solution.py:22
  351.7 18.1 %scatter_fusion = f32[128,128,512]{2,1,0:T(8,128)} fusion(f32[128,128,512]{2,1,0:T(8,128)} %get-tuple-element.139, s32[32]{0:T(128)S(1)} %compare_select_fusion.8, f32[32,128,512]{2,1,0:T(8,128)} %fusion.21), kind=kCustom, calls=%fused_computation.5.clone.1 | custom fusion | flops 2097152 | bytes 25165952 | tf_op jit(solution)/shard_map/while/body/scatter-add | solution.py:24
  372.6 5.3 gather_fusion.4
  380.7 6.7 %fusion.21 = f32[32,128,512]{2,1,0:T(8,128)} fusion(bf16[32,128,512]{2,1,0:T(8,128)(2,1)} %gather_fusion.3, pred[32]{0:T(512)(128)(4,1)S(1)} %get-tuple-element.125, bf16[32,128,128]{2,1,0:T(8,128)(2,1)S(1)} %gather_fusion.4, pred[32]{0:T(512)(128)(4,1)S(1)} %get-tuple-element.126), kind=kOutput, calls=%fused_computation.6.clone.1 | convolution fusion | flops 539492352 | bytes 13631552 | tf_op jit(solution)/shard_map/while/body/gij,gjc->gic/dot_general | solution.py:22
  387.4 17.3 %scatter_fusion = f32[128,128,512]{2,1,0:T(8,128)} fusion(f32[128,128,512]{2,1,0:T(8,128)} %get-tuple-element.139, s32[32]{0:T(128)S(1)} %compare_select_fusion.8, f32[32,128,512]{2,1,0:T(8,128)} %fusion.21), kind=kCustom, calls=%fused_computation.5.clone.1 | custom fusion | flops 2097152 | bytes 25165952 | tf_op jit(solution)/shard_map/while/body/scatter-add | solution.py:24
  407.5 5.3 gather_fusion.4
  415.6 6.7 %fusion.21 = f32[32,128,512]{2,1,0:T(8,128)} fusion(bf16[32,128,512]{2,1,0:T(8,128)(2,1)} %gather_fusion.3, pred[32]{0:T(512)(128)(4,1)S(1)} %get-tuple-element.125, bf16[32,128,128]{2,1,0:T(8,128)(2,1)S(1)} %gather_fusion.4, pred[32]{0:T(512)(128)(4,1)S(1)} %get-tuple-element.126), kind=kOutput, calls=%fused_computation.6.clone.1 | convolution fusion | flops 539492352 | bytes 13631552 | tf_op jit(solution)/shard_map/while/body/gij,gjc->gic/dot_general | solution.py:22
  422.3 17.2 %scatter_fusion = f32[128,128,512]{2,1,0:T(8,128)} fusion(f32[128,128,512]{2,1,0:T(8,128)} %get-tuple-element.139, s32[32]{0:T(128)S(1)} %compare_select_fusion.8, f32[32,128,512]{2,1,0:T(8,128)} %fusion.21), kind=kCustom, calls=%fused_computation.5.clone.1 | custom fusion | flops 2097152 | bytes 25165952 | tf_op jit(solution)/shard_map/while/body/scatter-add | solution.py:24
  442.5 5.3 gather_fusion.4
  450.5 6.7 %fusion.21 = f32[32,128,512]{2,1,0:T(8,128)} fusion(bf16[32,128,512]{2,1,0:T(8,128)(2,1)} %gather_fusion.3, pred[32]{0:T(512)(128)(4,1)S(1)} %get-tuple-element.125, bf16[32,128,128]{2,1,0:T(8,128)(2,1)S(1)} %gather_fusion.4, pred[32]{0:T(512)(128)(4,1)S(1)} %get-tuple-element.126), kind=kOutput, calls=%fused_computation.6.clone.1 | convolution fusion | flops 539492352 | bytes 13631552 | tf_op jit(solution)/shard_map/while/body/gij,gjc->gic/dot_general | solution.py:22
  457.2 15.3 %scatter_fusion = f32[128,128,512]{2,1,0:T(8,128)} fusion(f32[128,128,512]{2,1,0:T(8,128)} %get-tuple-element.139, s32[32]{0:T(128)S(1)} %compare_select_fusion.8, f32[32,128,512]{2,1,0:T(8,128)} %fusion.21), kind=kCustom, calls=%fused_computation.5.clone.1 | custom fusion | flops 2097152 | bytes 25165952 | tf_op jit(solution)/shard_map/while/body/scatter-add | solution.py:24
  472.6 165.2 %reduce-scatter.2.cloned.1.call-done = f32[512,512]{1,0:T(8,128)} async-done(((f32[16384,512]{1,0:T(8,128)}), f32[512,512]{1,0:T(8,128)}) %reduce-scatter.2.cloned.1.call-update) | async-done | bytes 1048592 | tf_op jit(solution)/shard_map/reduce_scatter | solution.py:43
  (143 shorter events, 46.6 us)
Async XLA Ops:
  6.5 35.8 %all-gather.2.cloned.1.call-start = ((), (), s32[]{:S(2)}) async-start(), calls=%async_computation.1 | async-start | bytes 2621440 | tf_op jit(solution)/shard_map/all_gather | solution.py:40
  7.3 630.6 %reduce-scatter.2.cloned.1.call-start = ((), (), s32[]{:S(2)}) async-start(), calls=%async_computation.2 | async-start | bytes 34603008 | tf_op jit(solution)/shard_map/reduce_scatter | solution.py:43
  42.3 11.3 %copy-start = (bf16[2048,512]{1,0:T(8,128)(2,1)S(1)}, bf16[2048,512]{1,0:T(8,128)(2,1)}, u32[]{:S(2)}) copy-start(bf16[2048,512]{1,0:T(8,128)(2,1)} %all-gather.2.cloned.1.call-done) | copy-start | bytes 6291460
Sparse Core Ops, SparseCore 0:
  9.0 33.2 all-gather.1
  472.8 165.0 reduce-scatter.1
where the time goes:
time: 648 us; the launch traced here: 645 us
  other arithmetic  216 us (33%)
  waiting for transfers between devices  200 us (31%)
  local copies, waits for them, and re-layouts  134 us (21%)
  matrix products  80.6 us (12%)
  between operations  14.1 us (2%)
    scatter-add x12, other arithmetic, step(): return acc.at[target].add(prods, mode='drop')  207 us
    reduce_scatter x1, waiting for transfers between devices, shards(): lax.psum_scatter(partial_value.reshape(rgroup * blk, loads), 'dom', scatt...  165 us
    dot_general x12, matrix products, step(): jnp.einsum('gij,gjc->gic', tile_group, xgroup, preferred_element_type=jnp...  80.6 us
    gather x12, local copies, waits for them, and re-layouts, step(): tile_group = jnp.take(tiles, safe, axis=0)  63.9 us
    all_gather x1, waiting for transfers between devices, shards(): gathered = lax.all_gather(loads_in, 'blk', axis=0, tiled=True)  33.6 us
    gather x12, local copies, waits for them, and re-layouts, step(): xgroup = jnp.take(xblocks, where_x, axis=0)  32.8 us
  transfers between devices with their start and end apart: 2, of which 2 were waited for; matrix products, arithmetic and copies ran while one was open for 0% of the time, Pallas kernels for 0%

commit v1 on v0

v1 whole, which is shorter than its diff:
```python
import functools

import jax
import jax.numpy as jnp
from jax import lax
from jax.experimental import pallas as pl
from jax.experimental.pallas import tpu as pltpu
from jax.sharding import PartitionSpec as P

CHUNKS = 2
REL = (2, 1, 3, 0)
UNROLL = 8
VMEM_LIMIT = 16 * 2**20
ORDER = (
    ("far", 0), ("rest", 0), ("ring1", 0), ("far", 1), ("rest", 1), ("ring1", 1), ("ring2", 0), ("ring2", 1), ("ring3", 0), ("ring3", 1),
)
FINE = 16.0
TOP = 32752.0
GROUP_FLOPS = 4_400_000_000


def tables(tile_rows, tile_cols, tile_counts, pb, n_blk, n_dom):
    slots = tile_rows.shape[0]
    rgroup = pb * n_dom
    d = lax.axis_index("dom")
    px, py, core = d // 8, (d // 2) % 4, d % 2
    rel = jnp.array(REL, jnp.int32)

    def starts(core):
        u, v = jnp.where(core == 0, px, py), jnp.where(core == 0, py, px)
        q, p = (u + rel[:, None]) % 4, (v + rel[None, :]) % 4
        return jnp.where(core == 0, (q * 4 + p) * 2, (p * 4 + q) * 2 + 1).reshape(-1)

    order = jnp.concatenate([starts(1 - core), starts(core)])
    edge = jnp.arange(rgroup, dtype=jnp.int32)
    group = jnp.arange(n_dom, dtype=jnp.int32)
    pos = jnp.sum(jnp.where(order[None, :] == edge[:, None] // pb, group[None, :] * pb, 0), axis=1) + edge % pb
    slot = jnp.arange(slots, dtype=jnp.int32)
    rows = jnp.where(slot < tile_counts[0], tile_rows - lax.axis_index("blk") * rgroup, rgroup)
    behind = (tile_cols // pb // n_dom - lax.axis_index("blk")) % n_blk
    xcol = jnp.clip(behind * pb + tile_cols % pb, 0, n_blk * pb - 1)
    ptr = jnp.sum((rows[None, :] < edge[:, None]).astype(jnp.int32), axis=1)
    num = jnp.sum((rows[None, :] == edge[:, None]).astype(jnp.int32), axis=1)
    half = (num + 1) // 2
    off = jnp.sum(jnp.where(pos[None, :] < pos[:, None], half[None, :], 0), axis=1)
    bound = jnp.arange(n_dom + 1, dtype=jnp.int32) * pb
    bound = jnp.sum(jnp.where(pos[None, :] < bound[:, None], half[None, :], 0), axis=1)
    item = jnp.arange((slots + rgroup) // 2 + UNROLL, dtype=jnp.int32)
    hot = (off[None, :] <= item[:, None]) & (item[:, None] < (off + half)[None, :])
    pick = lambda v: jnp.sum(jnp.where(hot, v[None, :], 0), axis=1)
    first = jnp.clip(pick(ptr - 2 * off) + 2 * item, 0, slots - 1)
    paired = first + 1 < pick(ptr + num)
    second = jnp.where(paired, first + 1, first)
    at = lambda t: jnp.sum(jnp.where(t[:, None] == slot[None, :], xcol[None, :], 0), axis=1)
    parts = dict(bound=bound, row=pick(pos), first=first, second=second, xa=at(first))
    parts["xb"] = jnp.where(paired, at(second), n_blk * pb)
    where, n = {}, 0
    for k, v in parts.items():
        where[k] = n
        n += v.shape[0]
    return where, jnp.concatenate(list(parts.values())).astype(jnp.int32)


def scale_of(msg, groups, g):
    blk = msg[pl.ds(groups * 512, 16), :].astype(jnp.int32).astype(jnp.float32)
    at = lax.broadcasted_iota(jnp.int32, blk.shape, 0)
    e = jnp.sum(jnp.where(at == g, blk, 0.0), axis=0, keepdims=True)
    return jnp.exp2(e * (1 / FINE)) * (1 / TOP)


def loop(count, body):
    if count == 1:
        body(0)
    else:
        lax.fori_loop(0, count, lambda k, _: (body(k), 0)[1], 0)


def kernel(where, base, total, segs, nin, nwait, outs, tab, tiles, x, *refs):
    ins, out_refs = refs[:nin], refs[nin + nwait : nin + nwait + len(outs)]
    acc, sc = refs[nin + nwait + len(outs) :]
    width = x.shape[-1]

    for first, count, adds, _, _ in segs:

        def begin(k):
            scales = [scale_of(ins[i], n, m + k) for i, n, m in adds]
            for i in range(4):
                value = None
                for (ref, _, m), s in zip(adds, scales):
                    at = pl.ds(pl.multiple_of((m + k) * 512 + i * 128, 128), 128)
                    part = ins[ref][at, :].astype(jnp.int32).astype(jnp.float32) * s
                    value = part if value is None else value + part
                acc[(first + k) * 4 + i] = jnp.zeros(acc.shape[1:], jnp.float32) if value is None else value

        loop(count, begin)

    lo, hi = tab[where["bound"] + base], tab[where["bound"] + base + total]

    def body(j, _):
        done = []
        for n in range(UNROLL):
            t = lo + j * UNROLL + n
            row = jnp.where(t < hi, tab[where["row"] + t] - 4 * base, 4 * total)
            lhs = jnp.concatenate([tiles[tab[where["first"] + t]], tiles[tab[where["second"] + t]]], axis=1)
            rhs = jnp.concatenate([x[tab[where["xa"] + t]], x[tab[where["xb"] + t]]], axis=0)
            done.append((row, jnp.dot(lhs, rhs, preferred_element_type=jnp.float32)))
        for row, value in done:
            acc[row] += value
        return 0

    lax.fori_loop(0, (hi - lo + UNROLL - 1) >> (UNROLL.bit_length() - 1), body, 0)

    sublane = lax.broadcasted_iota(jnp.int32, (16, width), 0)
    for o, (_, quant) in enumerate(outs):
        if quant:
            sc[o] = jnp.zeros(sc.shape[1:], jnp.int32)
    for first, count, _, o, place in segs:

        def finish(k):
            out = out_refs[o]
            terms = [acc.at[(first + k) * 4 + i] for i in range(4)]
            if not outs[o][1]:
                for i in range(4):
                    out[pl.ds(i * 128, 128), :] = terms[i][...]
                return
            top = functools.reduce(jnp.maximum, [jnp.max(jnp.abs(t[...]), axis=0, keepdims=True) for t in terms])
            e = jnp.ceil(FINE * jnp.log2(jnp.maximum(top, 1e-30)))
            inv = jnp.exp2(e * (-1 / FINE)) * TOP
            for i in range(4):
                at = pl.ds(pl.multiple_of((place + k) * 512 + i * 128, 128), 128)
                out[at, :] = jnp.round(terms[i][...] * inv).astype(jnp.int32).astype(jnp.int16)
            sc[o] = jnp.where(sublane == place + k, e.astype(jnp.int32), sc[o])

        loop(count, finish)
    for o, (groups, quant) in enumerate(outs):
        if quant:
            out_refs[o][pl.ds(groups * 512, 16), :] = sc[o].astype(jnp.int16)


def products(name, where, tab, tiles, x, base, total, segs, ins, outs, wait):
    width = x.shape[-1]
    blk = tiles.shape[1]
    smem, vmem = pl.BlockSpec(memory_space=pltpu.SMEM), pl.BlockSpec(memory_space=pltpu.VMEM)
    shapes = [
        jax.ShapeDtypeStruct((n * 512 + 16, width), jnp.int16) if quant else jax.ShapeDtypeStruct((512, width), jnp.float32)
        for n, quant in outs
    ]
    return pl.pallas_call(
        functools.partial(kernel, where, base, total, segs, len(ins), len(wait), outs),
        out_shape=shapes,
        in_specs=[smem] + [vmem] * (2 + len(ins)) + [pl.BlockSpec(memory_space=pl.ANY)] * len(wait),
        out_specs=[vmem] * len(outs),
        scratch_shapes=[
            pltpu.VMEM((4 * total + 1, blk, width), jnp.float32),
            pltpu.VMEM((len(outs), 16, width), jnp.int32),
        ],
        compiler_params=pltpu.CompilerParams(vmem_limit_bytes=VMEM_LIMIT),
        cost_estimate=pl.CostEstimate(flops=total * GROUP_FLOPS, bytes_accessed=1000, transcendentals=0),
        name=name,
    )(tab, tiles, x, *ins, *wait)


def join_kernel(n, nwait, *refs):
    out, at = refs[-1], 0
    for part in refs[:n]:
        out[pl.ds(at, part.shape[0])] = part[...]
        at += part.shape[0]
    out[pl.ds(at, out.shape[0] - at)] = jnp.zeros((out.shape[0] - at, *out.shape[1:]), out.dtype)


def join(name, parts, blk, wait):
    parts = [p.reshape(-1, blk, p.shape[-1]) for p in parts]
    total = sum(p.shape[0] for p in parts)
    return pl.pallas_call(
        functools.partial(join_kernel, len(parts), len(wait)),
        out_shape=jax.ShapeDtypeStruct((total + 1, *parts[0].shape[1:]), parts[0].dtype),
        in_specs=[pl.BlockSpec(memory_space=pltpu.VMEM)] * len(parts) + [pl.BlockSpec(memory_space=pl.ANY)] * len(wait),
        out_specs=pl.BlockSpec(memory_space=pltpu.VMEM),
        compiler_params=pltpu.CompilerParams(vmem_limit_bytes=VMEM_LIMIT),
        cost_estimate=pl.CostEstimate(flops=1000, bytes_accessed=1000, transcendentals=0),
        name=name,
    )(*parts, *wait)


def hold_kernel(src, dst, sem):
    copy = pltpu.make_async_copy(src, dst, sem)
    copy.start()
    copy.wait()


def hold(value):
    return pl.pallas_call(
        hold_kernel,
        out_shape=jax.ShapeDtypeStruct(value.shape, value.dtype),
        in_specs=[pl.BlockSpec(memory_space=pltpu.HBM)],
        out_specs=pl.BlockSpec(memory_space=pltpu.VMEM),
        scratch_shapes=[pltpu.SemaphoreType.DMA],
        compiler_params=pltpu.CompilerParams(vmem_limit_bytes=VMEM_LIMIT),
        cost_estimate=pl.CostEstimate(flops=GROUP_FLOPS, bytes_accessed=1000, transcendentals=0),
        name="hold",
    )(value)


def add_up_kernel(n, nwait, *refs):
    out = refs[-1]
    for j in range(n):
        own, *got = refs[4 * j : 4 * j + 4]
        width = own.shape[1]
        scales = [scale_of(m, 1, 0) for m in got]

        def some(i, _):
            at = pl.ds(pl.multiple_of(i * 128, 128), 128)
            value = own[at, :]
            for m, s in zip(got, scales):
                value = value + m[at, :].astype(jnp.int32).astype(jnp.float32) * s
            out[at, j * width : (j + 1) * width] = value
            return 0

        lax.fori_loop(0, own.shape[0] // 128, some, 0)


def add_up(parts, wait):
    rows, width = parts[0][0].shape
    flat = [p for part in parts for p in part]
    return pl.pallas_call(
        functools.partial(add_up_kernel, len(parts), len(wait)),
        out_shape=jax.ShapeDtypeStruct((rows, width * len(parts)), jnp.float32),
        in_specs=[pl.BlockSpec(memory_space=pltpu.VMEM)] * len(flat) + [pl.BlockSpec(memory_space=pl.ANY)] * len(wait),
        out_specs=pl.BlockSpec(memory_space=pltpu.VMEM),
        compiler_params=pltpu.CompilerParams(vmem_limit_bytes=VMEM_LIMIT),
        name="add_up",
    )(*flat, *wait)


def shards(tiles, tile_rows, tile_cols, tile_counts, loads_in):
    blk, loads = tiles.shape[1], loads_in.shape[1]
    pb = loads_in.shape[0] // blk
    n_blk, n_dom = lax.axis_size("blk"), lax.axis_size("dom")
    where, tab = tables(tile_rows, tile_cols, tile_counts, pb, n_blk, n_dom)
    width = loads // CHUNKS

    place = lambda x, y, c: (x % 4 * 4 + y % 4) * 2 + c
    every = [(x, y, c) for x in range(4) for y in range(4) for c in range(2)]
    pair = [(place(x, y, c), place(x, y, 1 - c)) for x, y, c in every]
    along = lambda k, axis: [
        (place(x, y, c), place(x + k, y, c) if c == axis else place(x, y + k, c)) for x, y, c in every
    ]
    send = lambda value, pairs: lax.ppermute(value, "dom", pairs)

    tiles = hold(tiles)
    ring = lambda k: [(i, (i - k) % n_blk) for i in range(n_blk)]
    parts = []
    for j in range(CHUNKS):
        part = loads_in[:, j * width : (j + 1) * width]
        others = [lax.ppermute(part, "blk", ring(k)) for k in (1, n_blk - 1, *range(2, n_blk - 1))]
        others.insert(n_blk - 2, others.pop(1))
        parts.append([part, *others])
    last, xs = [], {}

    def run(name, j, wait=(), **how):
        if j not in xs:
            xs[j] = join(f"join_{j}", parts[j], blk, list(last))
        value = products(f"{name}_{j}", where, tab, tiles, xs[j], wait=[*last, *wait], **how)
        last[:] = [value[-1]]
        return value

    kept = [{} for _ in range(CHUNKS)]

    def far(j, k):
        [a] = run("far", j, base=0, total=4, segs=[(0, 4, [], 0, 0)], ins=[], outs=[(4, True)])
        k["p1"] = send(a, pair)

    def ring1(j, k):
        h1, h2 = run(
            "ring1", j, wait=kept[j - 1]["r"] if j else (), base=16, total=4, ins=[k["p1"]], outs=[(2, True), (2, True)],
            segs=[(0, 2, [(0, 4, 0)], 0, 0), (2, 2, [(0, 4, 2)], 1, 0)],
        )
        k["r"] = send(h1, along(1, 0)), send(h2, along(-1, 0))

    def rest(j, k):
        [a] = run("rest", j, base=4, total=12, segs=[(0, 12, [], 0, 0)], ins=[], outs=[(12, True)])
        k["p2"] = send(a, pair)

    def ring2(j, k):
        m1, m2 = run(
            "ring2", j, base=20, total=8, ins=[k["p2"], *k["r"]], outs=[(4, True), (4, True)],
            segs=[
                (0, 2, [(0, 12, 0), (1, 2, 0)], 0, 0),
                (2, 2, [(0, 12, 2)], 0, 2),
                (4, 2, [(0, 12, 4)], 1, 0),
                (6, 2, [(0, 12, 6), (2, 2, 0)], 1, 2),
            ],
        )
        k["n"] = send(m1, along(1, 0)), send(m2, along(-1, 0))

    def ring3(j, k):
        t0, t1, t2, own = run(
            "ring3", j, base=28, total=4, ins=[k["p2"], *k["n"]], outs=[(1, True), (1, True), (1, True), (1, False)],
            segs=[(g, 1, [(0, 12, 8 + g), (1, 4, g), (2, 4, g)], g, 0) for g in range(4)],
        )
        k["t"] = own, [send(t0, along(2, 1)), send(t1, along(1, 1)), send(t2, along(-1, 1))]

    for step, j in ORDER:
        dict(far=far, ring1=ring1, rest=rest, ring2=ring2, ring3=ring3)[step](j, kept[j])
    return add_up([[k["t"][0], *k["t"][1]] for k in kept], last)


def solution(mesh):
    in_specs = (
        P(("blk", "dom"), None, None),
        P(("blk", "dom")),
        P(("blk", "dom")),
        P(("blk", "dom")),
        P(("blk", "dom"), None),
    )
    out_specs = P(("blk", "dom"), None)
    return jax.shard_map(shards, mesh=mesh, in_specs=in_specs, out_specs=out_specs, check_vma=False)
```

time: 648 us -> 110 us (0.17)
  other arithmetic: 216 us -> 1.38 us
  waiting for transfers between devices: 200 us -> 39.6 us
  local copies, waits for them, and re-layouts: 134 us -> 5.93 us
  matrix products: 80.6 us -> 0 us
  Pallas kernels: 0 us -> 34.2 us
  starting transfers between devices: 0.04 us -> 27.8 us
  between operations: 14.1 us -> 0.96 us
    scatter-add x12 -> x0, other arithmetic: 207 us -> none  [step(): return acc.at[target].add(prods, mode='drop')]
    reduce_scatter x1 -> x0, waiting for transfers between devices: 165 us -> none  [shards(): lax.psum_scatter(partial_value.reshape(rgroup * blk, loads), 'dom', scatt...]
    gather x60 -> x0, local copies, waits for them, and re-layouts: 122 us -> none  [the longest x12 63.9 us: step(): tile_group = jnp.take(tiles, safe, axis=0)]
    dot_general x12 -> x0, matrix products: 80.6 us -> none  [step(): jnp.einsum('gij,gjc->gic', tile_group, xgroup, preferred_element_type=jnp...]
    ppermute x0 -> x24, waiting for transfers between devices: none -> 39.6 us  [the longest x18 37.3 us: shards(): send = lambda value, pairs: lax.ppermute(value, 'dom', pairs)]
    pallas_call x0 -> x14, Pallas kernels: none -> 34.2 us  [the longest x10 31.7 us: products(): pl.pallas_call(functools.partial(kernel, where, base, total, segs, len(in...]
    all_gather x1 -> x0, waiting for transfers between devices: 33.6 us -> none  [shards(): gathered = lax.all_gather(loads_in, 'blk', axis=0, tiled=True)]
    ppermute x0 -> x24, starting transfers between devices: none -> 27.8 us  [the longest x18 18 us: shards(): send = lambda value, pairs: lax.ppermute(value, 'dom', pairs)]
  transfers between devices with their start and end apart: 2 -> 24, of which waited for: 2 -> 10; matrix products, arithmetic and copies ran while one was open for 0% -> 1% of each run, Pallas kernels for 0% -> 30%
where the time goes in v1:
time: 110 us
  waiting for transfers between devices  39.6 us (36%)
  Pallas kernels  34.2 us (31%)
  starting transfers between devices  27.8 us (25%)
  local copies, waits for them, and re-layouts  5.93 us (5%)
  other arithmetic  1.38 us (1%)
    ppermute x18, waiting for transfers between devices, shards(): send = lambda value, pairs: lax.ppermute(value, 'dom', pairs)  37.3 us
    pallas_call x10, Pallas kernels, products(): pl.pallas_call(functools.partial(kernel, where, base, total, segs, len(in...  31.7 us
    ppermute x18, starting transfers between devices, shards(): send = lambda value, pairs: lax.ppermute(value, 'dom', pairs)  18 us
    ppermute x6, starting transfers between devices, shards(): lax.ppermute(part, 'blk', ring(k))  9.74 us
    unnamed x8, local copies, waits for them, and re-layouts  4.58 us
    ppermute x6, waiting for transfers between devices, shards(): lax.ppermute(part, 'blk', ring(k))  2.25 us
  transfers between devices with their start and end apart: 24, of which 10 were waited for; matrix products, arithmetic and copies ran while one was open for 1% of the time, Pallas kernels for 30%

profile of v1, /device:TPU:14, one launch (start us, length us, event | category | flops | bytes accessed | tf_op | source)
XLA Modules:
  0.0 109.8 jit_solution(5945658209715102183)
XLA Ops:
  0.0 1.1 %fusion.14 = (bf16[512,256]{1,0:T(8,128)(2,1)S(1)}, bf16[512,256]{1,0:T(8,128)(2,1)S(1)}) fusion(bf16[512,512]{1,0:T(8,128)(2,1)} %param.10), kind=kLoop, calls=%fused_computation.81 | loop fusion | bytes 1048576 | tf_op jit(solution)/shard_map/slice | solution.py:254
  1.1 4.1 %collective-permute-start = (bf16[512,256]{1,0:T(8,128)(2,1)S(1)}, bf16[512,256]{1,0:T(8,128)(2,1)S(1)}, u32[]{:S(2)}, u32[]{:S(2)}) collective-permute-start(bf16[512,256]{1,0:T(8,128)(2,1)S(1)} %get-tuple-element.55), channel_id=1, source_target_pairs={{0,96},{32,0},{64,32},{96,64},{1,97},{33,1},{65,33},{97,65},{2,98}... | collective-permute-start | bytes 786440 | tf_op jit(solution)/shard_map/ppermute | solution.py:255
  5.2 1.3 %collective-permute-start.2 = (bf16[512,256]{1,0:T(8,128)(2,1)S(1)}, bf16[512,256]{1,0:T(8,128)(2,1)S(1)}, u32[]{:S(2)}, u32[]{:S(2)}) collective-permute-start(bf16[512,256]{1,0:T(8,128)(2,1)S(1)} %get-tuple-element.55), channel_id=1, source_target_pairs={{0,32},{32,64},{64,96},{96,0},{1,33},{33,65},{65,97},{97,1},{2,34}... | collective-permute-start | bytes 786440 | tf_op jit(solution)/shard_map/ppermute | solution.py:255
  6.5 2.0 %collective-permute-start.7 = (bf16[512,256]{1,0:T(8,128)(2,1)S(1)}, bf16[512,256]{1,0:T(8,128)(2,1)S(1)}, u32[]{:S(2)}, u32[]{:S(2)}) collective-permute-start(bf16[512,256]{1,0:T(8,128)(2,1)S(1)} %get-tuple-element.54), channel_id=1, source_target_pairs={{0,96},{32,0},{64,32},{96,64},{1,97},{33,1},{65,33},{97,65},{2,98}... | collective-permute-start | bytes 786440 | tf_op jit(solution)/shard_map/ppermute | solution.py:255
  8.5 2.3 %collective-permute-start.8 = (bf16[512,256]{1,0:T(8,128)(2,1)S(1)}, bf16[512,256]{1,0:T(8,128)(2,1)S(1)}, u32[]{:S(2)}, u32[]{:S(2)}) collective-permute-start(bf16[512,256]{1,0:T(8,128)(2,1)S(1)} %get-tuple-element.54), channel_id=1, source_target_pairs={{0,64},{32,96},{64,0},{96,32},{1,65},{33,97},{65,1},{97,33},{2,66}... | collective-permute-start | bytes 786440 | tf_op jit(solution)/shard_map/ppermute | solution.py:255
  10.9 0.1 select_n.185
  11.1 0.1 select_reduce_fusion.7
  11.9 0.1 convert_reduce_fusion
  12.1 0.2 select_reduce_fusion.5
  12.3 0.2 select_reduce_fusion.6
  12.5 0.3 select_reduce_fusion.2
  12.8 0.3 select_reduce_fusion
  13.0 0.1 concatenate.7.tab
  13.1 4.6 %copy-done = bf16[384,128,128]{2,1,0:T(8,128)(2,1)S(1)} copy-done((bf16[384,128,128]{2,1,0:T(8,128)(2,1)S(1)}, bf16[384,128,128]{2,1,0:T(8,128)(2,1)}, u32[]{:S(2)}) %copy-start) | copy-done | bytes 12582936
  17.7 0.8 hold.1.tiles
  18.7 2.2 %collective-permute-done.2 = bf16[512,256]{1,0:T(8,128)(2,1)S(1)} collective-permute-done((bf16[512,256]{1,0:T(8,128)(2,1)S(1)}, bf16[512,256]{1,0:T(8,128)(2,1)S(1)}, u32[]{:S(2)}, u32[]{:S(2)}) %collective-permute-start.2) | collective-permute-done | bytes 262176 | tf_op jit(solution)/shard_map/ppermute | solution.py:255
  21.0 2.2 %far_0.1.refs_0_ = s16[2064,256]{1,0:T(8,128)(2,1)S(1)} custom-call(s32[1353]{0:T(1024)S(1)} %concatenate.7.tab, bf16[384,128,128]{2,1,0:T(8,128)(2,1)S(1)} %hold.1.tiles, bf16[17,128,256]{2,1,0:T(8,128)(2,1)S(1)} %join_0.1.x), custom_call_target="tpu_custom_call" | custom-call | flops 17600000000 | bytes 1000 | tf_op jit(solution)/shard_map/far_0/pallas_call | solution.py:148
  23.2 0.1 collective-permute-start.4
  23.3 5.0 %rest_0.1.refs_1_ = s16[6160,256]{1,0:T(8,128)(2,1)S(1)} custom-call(s32[1353]{0:T(1024)S(1)} %concatenate.7.tab, bf16[384,128,128]{2,1,0:T(8,128)(2,1)S(1)} %hold.1.tiles, bf16[17,128,256]{2,1,0:T(8,128)(2,1)S(1)} %join_0.1.x, s16[2064,256]{1,0:T(8,128)(2,1)S(1)} %far_0.1.refs_0_), custom_call_target="tpu_custom_call" | custom-call | flops 52800000000 | bytes 1000 | tf_op jit(solution)/shard_map/rest_0/pallas_call | solution.py:148
  28.3 1.6 %collective-permute-start.3 = (s16[6160,256]{1,0:T(8,128)(2,1)S(1)}, s16[6160,256]{1,0:T(8,128)(2,1)S(1)}, u32[]{:S(2)}, u32[]{:S(2)}) collective-permute-start(s16[6160,256]{1,0:T(8,128)(2,1)S(1)} %rest_0.1.refs_1_), channel_id=1, source_target_pairs={{0,1},{1,0},{2,3},{3,2},{4,5},{5,4},{6,7},{7,6},{8,9},{9,8},{10,11... | collective-permute-start | bytes 9461768 | tf_op jit(solution)/shard_map/ppermute | solution.py:248
  29.8 2.0 %ring1_0.1 = (s16[1040,256]{1,0:T(8,128)(2,1)S(1)}, s16[1040,256]{1,0:T(8,128)(2,1)S(1)}) custom-call(s32[1353]{0:T(1024)S(1)} %concatenate.7.tab, bf16[384,128,128]{2,1,0:T(8,128)(2,1)S(1)} %hold.1.tiles, bf16[17,128,256]{2,1,0:T(8,128)(2,1)S(1)} %join_0.1.x, s16[2064,256]{1,0:T(8,128)(2,1)S(1)} %collective-permute-done.4.refs_0_, ...), custom_call_target="tpu_custom_call" | custom-call | flops 17600000000 | bytes 1000 | tf_op jit(solution)/shard_map/ring1_0/pallas_call | solution.py:148
  32.0 2.2 %far_1.1.refs_0_ = s16[2064,256]{1,0:T(8,128)(2,1)S(1)} custom-call(s32[1353]{0:T(1024)S(1)} %concatenate.7.tab, bf16[384,128,128]{2,1,0:T(8,128)(2,1)S(1)} %hold.1.tiles, bf16[17,128,256]{2,1,0:T(8,128)(2,1)S(1)} %join_1.1.x, s16[1040,256]{1,0:T(8,128)(2,1)S(1)} %get-tuple-element.22.refs_4_.refs_0_), custom_call_target="tpu_custom_call" | custom-call | flops 17600000000 | bytes 1000 | tf_op jit(solution)/shard_map/far_1/pallas_call | solution.py:148
  34.2 1.1 collective-permute-start.10
  35.3 1.9 %collective-permute-start.5 = (s16[1040,256]{1,0:T(8,128)(2,1)S(1)}, s16[1040,256]{1,0:T(8,128)(2,1)S(1)}, u32[]{:S(2)}, u32[]{:S(2)}) collective-permute-start(s16[1040,256]{1,0:T(8,128)(2,1)S(1)} %get-tuple-element.21), channel_id=1, source_target_pairs={{0,8},{1,3},{2,10},{3,5},{4,12},{5,7},{6,14},{7,1},{8,16},{9,11},{... | collective-permute-start | bytes 1597448 | tf_op jit(solution)/shard_map/ppermute | solution.py:248
  37.3 5.0 %rest_1.1.refs_1_ = s16[6160,256]{1,0:T(8,128)(2,1)S(1)} custom-call(s32[1353]{0:T(1024)S(1)} %concatenate.7.tab, bf16[384,128,128]{2,1,0:T(8,128)(2,1)S(1)} %hold.1.tiles, bf16[17,128,256]{2,1,0:T(8,128)(2,1)S(1)} %join_1.1.x, s16[2064,256]{1,0:T(8,128)(2,1)S(1)} %far_1.1.refs_0_), custom_call_target="tpu_custom_call" | custom-call | flops 52800000000 | bytes 1000 | tf_op jit(solution)/shard_map/rest_1/pallas_call | solution.py:148
  42.3 0.1 collective-permute-start.13
  42.4 2.2 %collective-permute-done.5.refs_2_.refs_1_ = s16[1040,256]{1,0:T(8,128)(2,1)S(1)} collective-permute-done((s16[1040,256]{1,0:T(8,128)(2,1)S(1)}, s16[1040,256]{1,0:T(8,128)(2,1)S(1)}, u32[]{:S(2)}, u32[]{:S(2)}) %collective-permute-start.5) | collective-permute-done | bytes 532512 | tf_op jit(solution)/shard_map/ppermute | solution.py:248
  44.6 2.0 %ring1_1.1 = (s16[1040,256]{1,0:T(8,128)(2,1)S(1)}, s16[1040,256]{1,0:T(8,128)(2,1)S(1)}) custom-call(s32[1353]{0:T(1024)S(1)} %concatenate.7.tab, bf16[384,128,128]{2,1,0:T(8,128)(2,1)S(1)} %hold.1.tiles, bf16[17,128,256]{2,1,0:T(8,128)(2,1)S(1)} %join_1.1.x, s16[2064,256]{1,0:T(8,128)(2,1)S(1)} %collective-permute-done.10.refs_0_, ...), custom_call_target="tpu_custom_call" | custom-call | flops 17600000000 | bytes 1000 | tf_op jit(solution)/shard_map/ring1_1/pallas_call | solution.py:148
  46.6 3.2 %collective-permute-start.14 = (s16[1040,256]{1,0:T(8,128)(2,1)S(1)}, s16[1040,256]{1,0:T(8,128)(2,1)S(1)}, u32[]{:S(2)}, u32[]{:S(2)}) collective-permute-start(s16[1040,256]{1,0:T(8,128)(2,1)S(1)} %get-tuple-element.26), channel_id=1, source_target_pairs={{0,8},{1,3},{2,10},{3,5},{4,12},{5,7},{6,14},{7,1},{8,16},{9,11},{... | collective-permute-start | bytes 1597448 | tf_op jit(solution)/shard_map/ppermute | solution.py:248
  49.8 3.9 %ring2_0.1 = (s16[2064,256]{1,0:T(8,128)(2,1)S(1)}, s16[2064,256]{1,0:T(8,128)(2,1)S(1)}) custom-call(s32[1353]{0:T(1024)S(1)} %concatenate.7.tab, bf16[384,128,128]{2,1,0:T(8,128)(2,1)S(1)} %hold.1.tiles, bf16[17,128,256]{2,1,0:T(8,128)(2,1)S(1)} %join_0.1.x, s16[6160,256]{1,0:T(8,128)(2,1)S(1)} %collective-permute-done.3.refs_0_, ...), custom_call_target="tpu_custom_call" | custom-call | flops 35200000000 | bytes 1000 | tf_op jit(solution)/shard_map/ring2_0/pallas_call | solution.py:148
  53.7 3.3 %collective-permute-start.11 = (s16[2064,256]{1,0:T(8,128)(2,1)S(1)}, s16[2064,256]{1,0:T(8,128)(2,1)S(1)}, u32[]{:S(2)}, u32[]{:S(2)}) collective-permute-start(s16[2064,256]{1,0:T(8,128)(2,1)S(1)} %get-tuple-element.24), channel_id=1, source_target_pairs={{0,8},{1,3},{2,10},{3,5},{4,12},{5,7},{6,14},{7,1},{8,16},{9,11},{... | collective-permute-start | bytes 3170312 | tf_op jit(solution)/shard_map/ppermute | solution.py:248
  57.0 3.2 %collective-permute-done.15.refs_2_ = s16[1040,256]{1,0:T(8,128)(2,1)S(1)} collective-permute-done((s16[1040,256]{1,0:T(8,128)(2,1)S(1)}, s16[1040,256]{1,0:T(8,128)(2,1)S(1)}, u32[]{:S(2)}, u32[]{:S(2)}) %collective-permute-start.15) | collective-permute-done | bytes 532512 | tf_op jit(solution)/shard_map/ppermute | solution.py:248
  60.3 4.1 %ring2_1.1 = (s16[2064,256]{1,0:T(8,128)(2,1)S(1)}, s16[2064,256]{1,0:T(8,128)(2,1)S(1)}) custom-call(s32[1353]{0:T(1024)S(1)} %concatenate.7.tab, bf16[384,128,128]{2,1,0:T(8,128)(2,1)S(1)} %hold.1.tiles, bf16[17,128,256]{2,1,0:T(8,128)(2,1)S(1)} %join_1.1.x, s16[6160,256]{1,0:T(8,128)(2,1)S(1)} %collective-permute-done.13.refs_0_, ...), custom_call_target="tpu_custom_call" | custom-call | flops 35200000000 | bytes 1000 | tf_op jit(solution)/shard_map/ring2_1/pallas_call | solution.py:148
  64.5 2.0 %collective-permute-start.20 = (s16[2064,256]{1,0:T(8,128)(2,1)S(1)}, s16[2064,256]{1,0:T(8,128)(2,1)S(1)}, u32[]{:S(2)}, u32[]{:S(2)}) collective-permute-start(s16[2064,256]{1,0:T(8,128)(2,1)S(1)} %get-tuple-element.27.refs_3_), channel_id=1, source_target_pairs={{0,24},{1,7},{2,26},{3,1},{4,28},{5,3},{6,30},{7,5},{8,0},{9,15},{... | collective-permute-start | bytes 3170312 | tf_op jit(solution)/shard_map/ppermute | solution.py:248
  66.5 3.0 %collective-permute-done.11.refs_1_ = s16[2064,256]{1,0:T(8,128)(2,1)S(1)} collective-permute-done((s16[2064,256]{1,0:T(8,128)(2,1)S(1)}, s16[2064,256]{1,0:T(8,128)(2,1)S(1)}, u32[]{:S(2)}, u32[]{:S(2)}) %collective-permute-start.11) | collective-permute-done | bytes 1056800 | tf_op jit(solution)/shard_map/ppermute | solution.py:248
  69.4 3.7 %collective-permute-done.12.refs_2_ = s16[2064,256]{1,0:T(8,128)(2,1)S(1)} collective-permute-done((s16[2064,256]{1,0:T(8,128)(2,1)S(1)}, s16[2064,256]{1,0:T(8,128)(2,1)S(1)}, u32[]{:S(2)}, u32[]{:S(2)}) %collective-permute-start.12) | collective-permute-done | bytes 1056800 | tf_op jit(solution)/shard_map/ppermute | solution.py:248
  73.1 2.7 %ring3_0.1 = (s16[528,256]{1,0:T(8,128)(2,1)S(1)}, s16[528,256]{1,0:T(8,128)(2,1)S(1)}, s16[528,256]{1,0:T(8,128)(2,1)S(1)}, f32[512,256]{1,0:T(8,128)S(1)}) custom-call(s32[1353]{0:T(1024)S(1)} %concatenate.7.tab, bf16[384,128,128]{2,1,0:T(8,128)(2,1)S(1)} %hold.1.tiles, bf16[17,128,256]{2,1,0:T(8,128)(2,1)S(1)} %join_0.1.x, ...), custom_call_target="tpu_custom_call" | custom-call | flops 17600000000 | bytes 1000 | tf_op jit(solution)/shard_map/ring3_0/pallas_call | solution.py:148
  75.8 0.4 collective-permute-start.16
  76.2 2.0 %collective-permute-start.18 = (s16[528,256]{1,0:T(8,128)(2,1)S(1)}, s16[528,256]{1,0:T(8,128)(2,1)S(1)}, u32[]{:S(2)}, u32[]{:S(2)}) collective-permute-start(s16[528,256]{1,0:T(8,128)(2,1)S(1)} %get-tuple-element.31), channel_id=1, source_target_pairs={{0,6},{1,25},{2,0},{3,27},{4,2},{5,29},{6,4},{7,31},{8,14},{9,1},{... | collective-permute-start | bytes 811016 | tf_op jit(solution)/shard_map/ppermute | solution.py:248
  78.3 12.8 %collective-permute-done.19.refs_1_ = s16[2064,256]{1,0:T(8,128)(2,1)S(1)} collective-permute-done((s16[2064,256]{1,0:T(8,128)(2,1)S(1)}, s16[2064,256]{1,0:T(8,128)(2,1)S(1)}, u32[]{:S(2)}, u32[]{:S(2)}) %collective-permute-start.19) | collective-permute-done | bytes 1056800 | tf_op jit(solution)/shard_map/ppermute | solution.py:248
  91.1 3.6 %collective-permute-done.20.refs_2_ = s16[2064,256]{1,0:T(8,128)(2,1)S(1)} collective-permute-done((s16[2064,256]{1,0:T(8,128)(2,1)S(1)}, s16[2064,256]{1,0:T(8,128)(2,1)S(1)}, u32[]{:S(2)}, u32[]{:S(2)}) %collective-permute-start.20) | collective-permute-done | bytes 1056800 | tf_op jit(solution)/shard_map/ppermute | solution.py:248
  94.7 2.7 %ring3_1.1 = (s16[528,256]{1,0:T(8,128)(2,1)S(1)}, s16[528,256]{1,0:T(8,128)(2,1)S(1)}, s16[528,256]{1,0:T(8,128)(2,1)S(1)}, f32[512,256]{1,0:T(8,128)S(1)}) custom-call(s32[1353]{0:T(1024)S(1)} %concatenate.7.tab, bf16[384,128,128]{2,1,0:T(8,128)(2,1)S(1)} %hold.1.tiles, bf16[17,128,256]{2,1,0:T(8,128)(2,1)S(1)} %join_1.1.x, ...), custom_call_target="tpu_custom_call" | custom-call | flops 17600000000 | bytes 1000 | tf_op jit(solution)/shard_map/ring3_1/pallas_call | solution.py:148
  97.4 0.1 collective-permute-start.21
  97.6 2.0 %collective-permute-start.23 = (s16[528,256]{1,0:T(8,128)(2,1)S(1)}, s16[528,256]{1,0:T(8,128)(2,1)S(1)}, u32[]{:S(2)}, u32[]{:S(2)}) collective-permute-start(s16[528,256]{1,0:T(8,128)(2,1)S(1)} %get-tuple-element.36), channel_id=1, source_target_pairs={{0,6},{1,25},{2,0},{3,27},{4,2},{5,29},{6,4},{7,31},{8,14},{9,1},{... | collective-permute-start | bytes 811016 | tf_op jit(solution)/shard_map/ppermute | solution.py:248
  99.6 5.9 %collective-permute-done.21.refs_5_ = s16[528,256]{1,0:T(8,128)(2,1)S(1)} collective-permute-done((s16[528,256]{1,0:T(8,128)(2,1)S(1)}, s16[528,256]{1,0:T(8,128)(2,1)S(1)}, u32[]{:S(2)}, u32[]{:S(2)}) %collective-permute-start.21) | collective-permute-done | bytes 270368 | tf_op jit(solution)/shard_map/ppermute | solution.py:248
  105.5 1.2 %collective-permute-done.22.refs_6_ = s16[528,256]{1,0:T(8,128)(2,1)S(1)} collective-permute-done((s16[528,256]{1,0:T(8,128)(2,1)S(1)}, s16[528,256]{1,0:T(8,128)(2,1)S(1)}, u32[]{:S(2)}, u32[]{:S(2)}) %collective-permute-start.22) | collective-permute-done | bytes 270368 | tf_op jit(solution)/shard_map/ppermute | solution.py:248
  106.7 1.6 %collective-permute-done.23.refs_7_ = s16[528,256]{1,0:T(8,128)(2,1)S(1)} collective-permute-done((s16[528,256]{1,0:T(8,128)(2,1)S(1)}, s16[528,256]{1,0:T(8,128)(2,1)S(1)}, u32[]{:S(2)}, u32[]{:S(2)}) %collective-permute-start.23) | collective-permute-done | bytes 270368 | tf_op jit(solution)/shard_map/ppermute | solution.py:248
  108.3 1.4 %add_up.1 = f32[512,512]{1,0:T(8,128)} custom-call(f32[512,256]{1,0:T(8,128)S(1)} %get-tuple-element.28.refs_3_.refs_0_, s16[528,256]{1,0:T(8,128)(2,1)S(1)} %collective-permute-done.16.refs_1_, s16[528,256]{1,0:T(8,128)(2,1)S(1)} %collective-permute-done.17.refs_2_, s16[528,256]{1,0:T(8,128)(2,1)S(1)} %collective-permute-done.18.refs_3_, ...), custom_call_target="tpu_custom_call" | custom-call | tf_op jit(solution)/shard_map/add_up/pallas_call | solution.py:225
  (45 shorter events, 0.9 us)
Async XLA Ops:
  0.0 10.8 %copy-start.3 = (s32[4]{0:T(128)S(1)}, s32[4]{0:T(128)}, u32[]{:S(2)}) copy-start(s32[4]{0:T(128)} %constant.168.clone) | copy-start | bytes 52
  0.0 11.9 %copy-start.1 = (s32[384]{0:T(512)S(1)}, s32[384]{0:T(512)}, u32[]{:S(2)}) copy-start(s32[384]{0:T(512)} %param.7) | copy-start | bytes 4612
  0.0 12.1 %copy-start.2 = (s32[384]{0:T(512)S(1)}, s32[384]{0:T(512)}, u32[]{:S(2)}) copy-start(s32[384]{0:T(512)} %param.8) | copy-start | bytes 4612
  1.1 17.5 %collective-permute-start = (bf16[512,256]{1,0:T(8,128)(2,1)S(1)}, bf16[512,256]{1,0:T(8,128)(2,1)S(1)}, u32[]{:S(2)}, u32[]{:S(2)}) collective-permute-start(bf16[512,256]{1,0:T(8,128)(2,1)S(1)} %get-tuple-element.55), channel_id=1, source_target_pairs={{0,96},{32,0},{64,32},{96,64},{1,97},{33,1},{65,33},{97,65},{2,98}... | collective-permute-start | bytes 786440 | tf_op jit(solution)/shard_map/ppermute | solution.py:255
  5.2 13.4 %collective-permute-start.1 = (bf16[512,256]{1,0:T(8,128)(2,1)S(1)}, bf16[512,256]{1,0:T(8,128)(2,1)S(1)}, u32[]{:S(2)}, u32[]{:S(2)}) collective-permute-start(bf16[512,256]{1,0:T(8,128)(2,1)S(1)} %get-tuple-element.55), channel_id=1, source_target_pairs={{0,64},{32,96},{64,0},{96,32},{1,65},{33,97},{65,1},{97,33},{2,66}... | collective-permute-start | bytes 786440 | tf_op jit(solution)/shard_map/ppermute | solution.py:255
  5.2 15.7 %collective-permute-start.2 = (bf16[512,256]{1,0:T(8,128)(2,1)S(1)}, bf16[512,256]{1,0:T(8,128)(2,1)S(1)}, u32[]{:S(2)}, u32[]{:S(2)}) collective-permute-start(bf16[512,256]{1,0:T(8,128)(2,1)S(1)} %get-tuple-element.55), channel_id=1, source_target_pairs={{0,32},{32,64},{64,96},{96,0},{1,33},{33,65},{65,97},{97,1},{2,34}... | collective-permute-start | bytes 786440 | tf_op jit(solution)/shard_map/ppermute | solution.py:255
  6.5 25.4 %collective-permute-start.7 = (bf16[512,256]{1,0:T(8,128)(2,1)S(1)}, bf16[512,256]{1,0:T(8,128)(2,1)S(1)}, u32[]{:S(2)}, u32[]{:S(2)}) collective-permute-start(bf16[512,256]{1,0:T(8,128)(2,1)S(1)} %get-tuple-element.54), channel_id=1, source_target_pairs={{0,96},{32,0},{64,32},{96,64},{1,97},{33,1},{65,33},{97,65},{2,98}... | collective-permute-start | bytes 786440 | tf_op jit(solution)/shard_map/ppermute | solution.py:255
  8.5 23.5 %collective-permute-start.8 = (bf16[512,256]{1,0:T(8,128)(2,1)S(1)}, bf16[512,256]{1,0:T(8,128)(2,1)S(1)}, u32[]{:S(2)}, u32[]{:S(2)}) collective-permute-start(bf16[512,256]{1,0:T(8,128)(2,1)S(1)} %get-tuple-element.54), channel_id=1, source_target_pairs={{0,64},{32,96},{64,0},{96,32},{1,65},{33,97},{65,1},{97,33},{2,66}... | collective-permute-start | bytes 786440 | tf_op jit(solution)/shard_map/ppermute | solution.py:255
  13.1 4.6 %copy-start = (bf16[384,128,128]{2,1,0:T(8,128)(2,1)S(1)}, bf16[384,128,128]{2,1,0:T(8,128)(2,1)}, u32[]{:S(2)}) copy-start(bf16[384,128,128]{2,1,0:T(8,128)(2,1)} %src.1) | copy-start | bytes 37748740
  18.6 13.4 %collective-permute-start.9 = (bf16[512,256]{1,0:T(8,128)(2,1)S(1)}, bf16[512,256]{1,0:T(8,128)(2,1)S(1)}, u32[]{:S(2)}, u32[]{:S(2)}) collective-permute-start(bf16[512,256]{1,0:T(8,128)(2,1)S(1)} %get-tuple-element.54), channel_id=1, source_target_pairs={{0,32},{32,64},{64,96},{96,0},{1,33},{33,65},{65,97},{97,1},{2,34}... | collective-permute-start | bytes 786440 | tf_op jit(solution)/shard_map/ppermute | solution.py:255
  23.2 6.7 %collective-permute-start.4 = (s16[2064,256]{1,0:T(8,128)(2,1)S(1)}, s16[2064,256]{1,0:T(8,128)(2,1)S(1)}, u32[]{:S(2)}, u32[]{:S(2)}) collective-permute-start(s16[2064,256]{1,0:T(8,128)(2,1)S(1)} %far_0.1.refs_0_), channel_id=1, source_target_pairs={{0,1},{1,0},{2,3},{3,2},{4,5},{5,4},{6,7},{7,6},{8,9},{9,8},{10,11... | collective-permute-start | bytes 3170312 | tf_op jit(solution)/shard_map/ppermute | solution.py:248
  28.3 21.5 %collective-permute-start.3 = (s16[6160,256]{1,0:T(8,128)(2,1)S(1)}, s16[6160,256]{1,0:T(8,128)(2,1)S(1)}, u32[]{:S(2)}, u32[]{:S(2)}) collective-permute-start(s16[6160,256]{1,0:T(8,128)(2,1)S(1)} %rest_0.1.refs_1_), channel_id=1, source_target_pairs={{0,1},{1,0},{2,3},{3,2},{4,5},{5,4},{6,7},{7,6},{8,9},{9,8},{10,11... | collective-permute-start | bytes 9461768 | tf_op jit(solution)/shard_map/ppermute | solution.py:248
  31.8 12.8 %collective-permute-start.6 = (s16[1040,256]{1,0:T(8,128)(2,1)S(1)}, s16[1040,256]{1,0:T(8,128)(2,1)S(1)}, u32[]{:S(2)}, u32[]{:S(2)}) collective-permute-start(s16[1040,256]{1,0:T(8,128)(2,1)S(1)} %get-tuple-element.22.refs_4_.refs_0_), channel_id=1, source_target_pairs={{0,24},{1,7},{2,26},{3,1},{4,28},{5,3},{6,30},{7,5},{8,0},{9,15},{... | collective-permute-start | bytes 1597448 | tf_op jit(solution)/shard_map/ppermute | solution.py:248
  34.2 10.4 %collective-permute-start.10 = (s16[2064,256]{1,0:T(8,128)(2,1)S(1)}, s16[2064,256]{1,0:T(8,128)(2,1)S(1)}, u32[]{:S(2)}, u32[]{:S(2)}) collective-permute-start(s16[2064,256]{1,0:T(8,128)(2,1)S(1)} %far_1.1.refs_0_), channel_id=1, source_target_pairs={{0,1},{1,0},{2,3},{3,2},{4,5},{5,4},{6,7},{7,6},{8,9},{9,8},{10,11... | collective-permute-start | bytes 3170312 | tf_op jit(solution)/shard_map/ppermute | solution.py:248
  35.3 9.3 %collective-permute-start.5 = (s16[1040,256]{1,0:T(8,128)(2,1)S(1)}, s16[1040,256]{1,0:T(8,128)(2,1)S(1)}, u32[]{:S(2)}, u32[]{:S(2)}) collective-permute-start(s16[1040,256]{1,0:T(8,128)(2,1)S(1)} %get-tuple-element.21), channel_id=1, source_target_pairs={{0,8},{1,3},{2,10},{3,5},{4,12},{5,7},{6,14},{7,1},{8,16},{9,11},{... | collective-permute-start | bytes 1597448 | tf_op jit(solution)/shard_map/ppermute | solution.py:248
  42.3 18.0 %collective-permute-start.13 = (s16[6160,256]{1,0:T(8,128)(2,1)S(1)}, s16[6160,256]{1,0:T(8,128)(2,1)S(1)}, u32[]{:S(2)}, u32[]{:S(2)}) collective-permute-start(s16[6160,256]{1,0:T(8,128)(2,1)S(1)} %rest_1.1.refs_1_), channel_id=1, source_target_pairs={{0,1},{1,0},{2,3},{3,2},{4,5},{5,4},{6,7},{7,6},{8,9},{9,8},{10,11... | collective-permute-start | bytes 9461768 | tf_op jit(solution)/shard_map/ppermute | solution.py:248
  46.6 10.5 %collective-permute-start.14 = (s16[1040,256]{1,0:T(8,128)(2,1)S(1)}, s16[1040,256]{1,0:T(8,128)(2,1)S(1)}, u32[]{:S(2)}, u32[]{:S(2)}) collective-permute-start(s16[1040,256]{1,0:T(8,128)(2,1)S(1)} %get-tuple-element.26), channel_id=1, source_target_pairs={{0,8},{1,3},{2,10},{3,5},{4,12},{5,7},{6,14},{7,1},{8,16},{9,11},{... | collective-permute-start | bytes 1597448 | tf_op jit(solution)/shard_map/ppermute | solution.py:248
  49.8 10.5 %collective-permute-start.15 = (s16[1040,256]{1,0:T(8,128)(2,1)S(1)}, s16[1040,256]{1,0:T(8,128)(2,1)S(1)}, u32[]{:S(2)}, u32[]{:S(2)}) collective-permute-start(s16[1040,256]{1,0:T(8,128)(2,1)S(1)} %get-tuple-element.23.refs_3_), channel_id=1, source_target_pairs={{0,24},{1,7},{2,26},{3,1},{4,28},{5,3},{6,30},{7,5},{8,0},{9,15},{... | collective-permute-start | bytes 1597448 | tf_op jit(solution)/shard_map/ppermute | solution.py:248
  53.7 15.7 %collective-permute-start.11 = (s16[2064,256]{1,0:T(8,128)(2,1)S(1)}, s16[2064,256]{1,0:T(8,128)(2,1)S(1)}, u32[]{:S(2)}, u32[]{:S(2)}) collective-permute-start(s16[2064,256]{1,0:T(8,128)(2,1)S(1)} %get-tuple-element.24), channel_id=1, source_target_pairs={{0,8},{1,3},{2,10},{3,5},{4,12},{5,7},{6,14},{7,1},{8,16},{9,11},{... | collective-permute-start | bytes 3170312 | tf_op jit(solution)/shard_map/ppermute | solution.py:248
  57.0 16.1 %collective-permute-start.12 = (s16[2064,256]{1,0:T(8,128)(2,1)S(1)}, s16[2064,256]{1,0:T(8,128)(2,1)S(1)}, u32[]{:S(2)}, u32[]{:S(2)}) collective-permute-start(s16[2064,256]{1,0:T(8,128)(2,1)S(1)} %get-tuple-element.25.refs_3_), channel_id=1, source_target_pairs={{0,24},{1,7},{2,26},{3,1},{4,28},{5,3},{6,30},{7,5},{8,0},{9,15},{... | collective-permute-start | bytes 3170312 | tf_op jit(solution)/shard_map/ppermute | solution.py:248
  64.4 26.7 %collective-permute-start.19 = (s16[2064,256]{1,0:T(8,128)(2,1)S(1)}, s16[2064,256]{1,0:T(8,128)(2,1)S(1)}, u32[]{:S(2)}, u32[]{:S(2)}) collective-permute-start(s16[2064,256]{1,0:T(8,128)(2,1)S(1)} %get-tuple-element.32), channel_id=1, source_target_pairs={{0,8},{1,3},{2,10},{3,5},{4,12},{5,7},{6,14},{7,1},{8,16},{9,11},{... | collective-permute-start | bytes 3170312 | tf_op jit(solution)/shard_map/ppermute | solution.py:248
  64.5 30.2 %collective-permute-start.20 = (s16[2064,256]{1,0:T(8,128)(2,1)S(1)}, s16[2064,256]{1,0:T(8,128)(2,1)S(1)}, u32[]{:S(2)}, u32[]{:S(2)}) collective-permute-start(s16[2064,256]{1,0:T(8,128)(2,1)S(1)} %get-tuple-element.27.refs_3_), channel_id=1, source_target_pairs={{0,24},{1,7},{2,26},{3,1},{4,28},{5,3},{6,30},{7,5},{8,0},{9,15},{... | collective-permute-start | bytes 3170312 | tf_op jit(solution)/shard_map/ppermute | solution.py:248
  75.8 21.7 %collective-permute-start.16 = (s16[528,256]{1,0:T(8,128)(2,1)S(1)}, s16[528,256]{1,0:T(8,128)(2,1)S(1)}, u32[]{:S(2)}, u32[]{:S(2)}) collective-permute-start(s16[528,256]{1,0:T(8,128)(2,1)S(1)} %get-tuple-element.29), channel_id=1, source_target_pairs={{0,4},{1,17},{2,6},{3,19},{4,0},{5,21},{6,2},{7,23},{8,12},{9,25},... | collective-permute-start | bytes 811016 | tf_op jit(solution)/shard_map/ppermute | solution.py:248
  76.2 23.3 %collective-permute-start.17 = (s16[528,256]{1,0:T(8,128)(2,1)S(1)}, s16[528,256]{1,0:T(8,128)(2,1)S(1)}, u32[]{:S(2)}, u32[]{:S(2)}) collective-permute-start(s16[528,256]{1,0:T(8,128)(2,1)S(1)} %get-tuple-element.30), channel_id=1, source_target_pairs={{0,2},{1,9},{2,4},{3,11},{4,6},{5,13},{6,0},{7,15},{8,10},{9,17},{... | collective-permute-start | bytes 811016 | tf_op jit(solution)/shard_map/ppermute | solution.py:248
  76.2 23.3 %collective-permute-start.18 = (s16[528,256]{1,0:T(8,128)(2,1)S(1)}, s16[528,256]{1,0:T(8,128)(2,1)S(1)}, u32[]{:S(2)}, u32[]{:S(2)}) collective-permute-start(s16[528,256]{1,0:T(8,128)(2,1)S(1)} %get-tuple-element.31), channel_id=1, source_target_pairs={{0,6},{1,25},{2,0},{3,27},{4,2},{5,29},{6,4},{7,31},{8,14},{9,1},{... | collective-permute-start | bytes 811016 | tf_op jit(solution)/shard_map/ppermute | solution.py:248
  97.4 8.1 %collective-permute-start.21 = (s16[528,256]{1,0:T(8,128)(2,1)S(1)}, s16[528,256]{1,0:T(8,128)(2,1)S(1)}, u32[]{:S(2)}, u32[]{:S(2)}) collective-permute-start(s16[528,256]{1,0:T(8,128)(2,1)S(1)} %get-tuple-element.34), channel_id=1, source_target_pairs={{0,4},{1,17},{2,6},{3,19},{4,0},{5,21},{6,2},{7,23},{8,12},{9,25},... | collective-permute-start | bytes 811016 | tf_op jit(solution)/shard_map/ppermute | solution.py:248
  97.5 9.3 %collective-permute-start.22 = (s16[528,256]{1,0:T(8,128)(2,1)S(1)}, s16[528,256]{1,0:T(8,128)(2,1)S(1)}, u32[]{:S(2)}, u32[]{:S(2)}) collective-permute-start(s16[528,256]{1,0:T(8,128)(2,1)S(1)} %get-tuple-element.35), channel_id=1, source_target_pairs={{0,2},{1,9},{2,4},{3,11},{4,6},{5,13},{6,0},{7,15},{8,10},{9,17},{... | collective-permute-start | bytes 811016 | tf_op jit(solution)/shard_map/ppermute | solution.py:248
  97.6 10.8 %collective-permute-start.23 = (s16[528,256]{1,0:T(8,128)(2,1)S(1)}, s16[528,256]{1,0:T(8,128)(2,1)S(1)}, u32[]{:S(2)}, u32[]{:S(2)}) collective-permute-start(s16[528,256]{1,0:T(8,128)(2,1)S(1)} %get-tuple-element.36), channel_id=1, source_target_pairs={{0,6},{1,25},{2,0},{3,27},{4,2},{5,29},{6,4},{7,31},{8,14},{9,1},{... | collective-permute-start | bytes 811016 | tf_op jit(solution)/shard_map/ppermute | solution.py:248

commit v2 on v1

v2 whole, which is shorter than its diff:
```python
import functools

import jax
import jax.numpy as jnp
from jax import lax
from jax.experimental import pallas as pl
from jax.experimental.pallas import tpu as pltpu
from jax.sharding import PartitionSpec as P

SPLIT = (1, 1)
CHUNKS = len(SPLIT)
REL = (2, 1, 3, 0)
UNROLL = 8
VMEM_LIMIT = 14 * 2**20
PREP_LIMIT = 34 * 2**20
BOUND, ROW, FIRST, SECOND, XA, XB = range(6)
WAITS = {("far", 1): [("r", 0)]}
ORDER = (
    ("far", 0), ("ring1", 0), ("rest", 0), ("far", 1), ("rest", 1), ("ring1", 1), ("ring2", 0), ("ring2", 1), ("ring3", 0), ("ring3", 1),
)
FINE = 16.0
TOP = 32752.0
GROUP_FLOPS = 4400000000


def prepare_kernel(pb, n_dom, n_blk, info, src, rows, cols, tab, dst, sem):
    copy = pltpu.make_async_copy(src, dst, sem)
    copy.start()
    slots, rgroup = rows.shape[1], pb * n_dom
    iota = lambda shape, axis: lax.broadcasted_iota(jnp.int32, shape, axis)
    count, blk, px, py, core = info[0], info[1], info[2], info[3], info[4]

    def position(r):
        kind, y, x = (r >> 2) & 1, (r >> 3) & 3, r >> 5
        first = kind == 0
        u = (jnp.where(first, x, y) - jnp.where(first, px, py)) & 3
        v = (jnp.where(first, y, x) - jnp.where(first, py, px)) & 3
        place = lambda rel: functools.reduce(lambda w, i: jnp.where(rel == REL[i], i, w), range(3), jnp.full_like(rel, 3))
        return ((jnp.where(kind == core, n_dom // 2, 0) + place(u) * 4 + place(v)) * pb + (r & 3)).astype(jnp.float32)

    total = lambda mask, value, axis: jnp.sum(jnp.where(mask, value, 0.0), axis=axis, keepdims=True)
    item = iota((1, slots), 1)
    row = jnp.where(item < count, rows[...] - blk * rgroup, rgroup)
    col = cols[...]
    xcol = jnp.clip((((col >> 7) - blk) & (n_blk - 1)) * pb + (col & (pb - 1)), 0, n_blk * pb - 1).astype(jnp.float32)
    square = (slots, slots)
    down = iota(square, 0)
    turn = lambda v: total(down == iota(square, 1), v, 1)
    row_c, xcol_c = turn(row.astype(jnp.float32)), turn(xcol)
    r_l, r_c = iota((1, rgroup), 1), iota((rgroup, 1), 0)
    halved = lambda n: ((n.astype(jnp.int32) + 1) >> 1).astype(jnp.float32)
    half_l = halved(total(row_c == r_l.astype(jnp.float32), 1.0, 0))
    num_c = total(row == r_c, 1.0, 1)
    ptr_c = total(row < r_c, 1.0, 1)
    half_c = halved(num_c)
    pos_l, pos_c = position(r_l), position(r_c)
    off_c = total(pos_l < pos_c, half_l, 1)
    at = item.astype(jnp.float32)
    hot = (off_c <= at) & (at < off_c + half_c)
    first = jnp.clip(total(hot, ptr_c - 2.0 * off_c, 0) + 2.0 * at, 0.0, slots - 1.0)
    paired = first + 1.0 < total(hot, ptr_c + num_c, 0)
    second = jnp.where(paired, first + 1.0, first)
    down_f = down.astype(jnp.float32)
    of = lambda t: total(down_f == t, xcol_c, 0)
    lines = (
        total(pos_c < at * pb, half_c, 0), total(hot, pos_c, 0), first, second, of(first),
        jnp.where(paired, of(second), float(n_blk * pb)),
    )
    for i, line in enumerate(lines):
        tab[pl.ds(i, 1), :] = line.astype(jnp.int32)
    copy.wait()


def prepare(tiles, tile_rows, tile_cols, tile_counts, pb, n_blk, n_dom):
    slots = tile_rows.shape[0]
    d = lax.axis_index("dom")
    info = jnp.stack([tile_counts[0], lax.axis_index("blk"), d // 8, (d // 2) % 4, d % 2]).astype(jnp.int32)
    smem, vmem = pl.BlockSpec(memory_space=pltpu.SMEM), pl.BlockSpec(memory_space=pltpu.VMEM)
    return pl.pallas_call(
        functools.partial(prepare_kernel, pb, n_dom, n_blk),
        out_shape=[jax.ShapeDtypeStruct((8, slots), jnp.int32), jax.ShapeDtypeStruct(tiles.shape, tiles.dtype)],
        in_specs=[smem, pl.BlockSpec(memory_space=pltpu.HBM), vmem, vmem],
        out_specs=[vmem, vmem],
        scratch_shapes=[pltpu.SemaphoreType.DMA],
        compiler_params=pltpu.CompilerParams(vmem_limit_bytes=PREP_LIMIT),
        cost_estimate=pl.CostEstimate(flops=GROUP_FLOPS, bytes_accessed=1000, transcendentals=0),
        name="prepare",
    )(info, tiles, tile_rows.reshape(1, slots), tile_cols.reshape(1, slots))


def scale_of(msg, groups, g, at=0):
    blk = msg[pl.ds(at + groups * 512, 16), :].astype(jnp.int32).astype(jnp.float32)
    row = lax.broadcasted_iota(jnp.int32, blk.shape, 0)
    e = jnp.sum(jnp.where(row == g, blk, 0.0), axis=0, keepdims=True)
    return jnp.exp2(e * (1 / FINE)) * (1 / TOP)


def loop(count, body):
    if count == 1:
        body(0)
    else:
        lax.fori_loop(0, count, lambda k, _: (body(k), 0)[1], 0)


def kernel(base, total, segs, nin, nwait, outs, carry, tab, tiles, x, *refs):
    ins, out_refs = refs[:nin], refs[nin + nwait : nin + nwait + len(outs)]
    acc, sc = refs[nin + nwait + len(outs) :]
    width = x.shape[-1]

    for first, count, adds, _, _ in segs:

        def begin(k):
            scales = [scale_of(ins[i], n, m + k) for i, n, m in adds]
            for i in range(4):
                value = None
                for (ref, _, m), s in zip(adds, scales):
                    at = pl.ds(pl.multiple_of((m + k) * 512 + i * 128, 128), 128)
                    part = ins[ref][at, :].astype(jnp.int32).astype(jnp.float32) * s
                    value = part if value is None else value + part
                acc[(first + k) * 4 + i] = jnp.zeros(acc.shape[1:], jnp.float32) if value is None else value

        loop(count, begin)

    lo, hi = tab[BOUND, base], tab[BOUND, base + total]

    def body(j, _):
        done = []
        for n in range(UNROLL):
            t = lo + j * UNROLL + n
            row = jnp.where(t < hi, tab[ROW, t] - 4 * base, 4 * total)
            lhs = jnp.concatenate([tiles[tab[FIRST, t]], tiles[tab[SECOND, t]]], axis=1)
            rhs = jnp.concatenate([x[tab[XA, t]], x[tab[XB, t]]], axis=0)
            done.append((row, jnp.dot(lhs, rhs, preferred_element_type=jnp.float32)))
        for row, value in done:
            acc[row] += value
        return 0

    lax.fori_loop(0, (hi - lo + UNROLL - 1) >> (UNROLL.bit_length() - 1), body, 0)

    sublane = lax.broadcasted_iota(jnp.int32, (16, width), 0)
    for o, (_, quant) in enumerate(outs):
        if quant:
            sc[o] = jnp.zeros(sc.shape[1:], jnp.int32)
    for first, count, _, o, place in segs:

        def finish(k):
            out = out_refs[o]
            terms = [acc.at[(first + k) * 4 + i] for i in range(4)]
            if not outs[o][1]:
                for i in range(4):
                    out[pl.ds(i * 128, 128), :] = terms[i][...]
                return
            top = functools.reduce(jnp.maximum, [jnp.max(jnp.abs(t[...]), axis=0, keepdims=True) for t in terms])
            e = jnp.ceil(FINE * jnp.log2(jnp.maximum(top, 1e-30)))
            inv = jnp.exp2(e * (-1 / FINE)) * TOP
            for i in range(4):
                at = pl.ds(pl.multiple_of((place + k) * 512 + i * 128, 128), 128)
                out[at, :] = jnp.round(terms[i][...] * inv).astype(jnp.int32).astype(jnp.int16)
            sc[o] = jnp.where(sublane == place + k, e.astype(jnp.int32), sc[o])

        loop(count, finish)
    for o, (groups, quant) in enumerate(outs):
        if quant:
            out_refs[o][pl.ds(groups * 512, 16), :] = sc[o].astype(jnp.int16)
    for o in range(carry):
        more = ins[nin - carry + o]
        out_refs[o][pl.ds(outs[o][0] * 512 + 16, more.shape[0]), :] = more[...]


def products(name, tab, tiles, x, base, total, segs, ins, outs, wait, carry=0):
    width = x.shape[-1]
    blk = tiles.shape[1]
    smem, vmem = pl.BlockSpec(memory_space=pltpu.SMEM), pl.BlockSpec(memory_space=pltpu.VMEM)
    shapes = [
        jax.ShapeDtypeStruct((n * 512 + 16, width), jnp.int16) if quant else jax.ShapeDtypeStruct((512, width), jnp.float32)
        for n, quant in outs
    ]
    for o in range(carry):
        rows = shapes[o].shape[0] + ins[len(ins) - carry + o].shape[0]
        shapes[o] = jax.ShapeDtypeStruct((rows, width), jnp.int16)
    return pl.pallas_call(
        functools.partial(kernel, base, total, segs, len(ins), len(wait), outs, carry),
        out_shape=shapes,
        in_specs=[smem] + [vmem] * (2 + len(ins)) + [pl.BlockSpec(memory_space=pl.ANY)] * len(wait),
        out_specs=[vmem] * len(outs),
        scratch_shapes=[
            pltpu.VMEM((4 * total + 1, blk, width), jnp.float32),
            pltpu.VMEM((len(outs), 16, width), jnp.int32),
        ],
        compiler_params=pltpu.CompilerParams(vmem_limit_bytes=VMEM_LIMIT),
        cost_estimate=pl.CostEstimate(flops=total * GROUP_FLOPS, bytes_accessed=1000, transcendentals=0),
        name=name,
    )(tab, tiles, x, *ins, *wait)


def join_kernel(n, nwait, *refs):
    out, at = refs[-1], 0
    for part in refs[:n]:
        out[pl.ds(at, part.shape[0])] = part[...]
        at += part.shape[0]
    out[pl.ds(at, out.shape[0] - at)] = jnp.zeros((out.shape[0] - at, *out.shape[1:]), out.dtype)


def join(name, parts, blk, wait):
    parts = [p.reshape(-1, blk, p.shape[-1]) for p in parts]
    total = sum(p.shape[0] for p in parts)
    return pl.pallas_call(
        functools.partial(join_kernel, len(parts), len(wait)),
        out_shape=jax.ShapeDtypeStruct((total + 1, *parts[0].shape[1:]), parts[0].dtype),
        in_specs=[pl.BlockSpec(memory_space=pltpu.VMEM)] * len(parts) + [pl.BlockSpec(memory_space=pl.ANY)] * len(wait),
        out_specs=pl.BlockSpec(memory_space=pltpu.VMEM),
        compiler_params=pltpu.CompilerParams(vmem_limit_bytes=VMEM_LIMIT),
        cost_estimate=pl.CostEstimate(flops=1000, bytes_accessed=1000, transcendentals=0),
        name=name,
    )(*parts, *wait)


def add_up_kernel(n, ngot, *refs):
    owns, got, out = refs[:n], refs[n : n + ngot], refs[-1]
    left = 0
    for j, own in enumerate(owns):
        right, begin = left + own.shape[1], (n - 1 - j) * 528
        scales = [scale_of(m, 1, 0, begin) for m in got]
        for i in range(own.shape[0] // 128):
            value = own[i * 128 : (i + 1) * 128, :]
            for m, s in zip(got, scales):
                value = value + m[pl.ds(begin + i * 128, 128), :].astype(jnp.int32).astype(jnp.float32) * s
            out[i * 128 : (i + 1) * 128, left:right] = value
        left = right


def add_up(owns, got, wait):
    rows, width = owns[0].shape[0], sum(own.shape[1] for own in owns)
    vmem = pl.BlockSpec(memory_space=pltpu.VMEM)
    return pl.pallas_call(
        functools.partial(add_up_kernel, len(owns), len(got)),
        out_shape=jax.ShapeDtypeStruct((rows, width), jnp.float32),
        in_specs=[vmem] * (len(owns) + len(got)) + [pl.BlockSpec(memory_space=pl.ANY)] * len(wait),
        out_specs=vmem,
        compiler_params=pltpu.CompilerParams(vmem_limit_bytes=VMEM_LIMIT),
        name="add_up",
    )(*owns, *got, *wait)


def shards(tiles, tile_rows, tile_cols, tile_counts, loads_in):
    blk, loads = tiles.shape[1], loads_in.shape[1]
    pb = loads_in.shape[0] // blk
    n_blk, n_dom = lax.axis_size("blk"), lax.axis_size("dom")
    tab, tiles = prepare(tiles, tile_rows, tile_cols, tile_counts, pb, n_blk, n_dom)
    edges = [loads * sum(SPLIT[:j]) // sum(SPLIT) for j in range(CHUNKS + 1)]

    place = lambda x, y, c: (x % 4 * 4 + y % 4) * 2 + c
    every = [(x, y, c) for x in range(4) for y in range(4) for c in range(2)]
    pair = [(place(x, y, c), place(x, y, 1 - c)) for x, y, c in every]
    along = lambda k, axis: [
        (place(x, y, c), place(x + k, y, c) if c == axis else place(x, y + k, c)) for x, y, c in every
    ]
    send = lambda value, pairs: lax.ppermute(value, "dom", pairs)

    ring = lambda k: [(i, (i - k) % n_blk) for i in range(n_blk)]
    parts = []
    for j in range(CHUNKS):
        part = loads_in[:, edges[j] : edges[j + 1]]
        others = [lax.ppermute(part, "blk", ring(k)) for k in (1, n_blk - 1, *range(2, n_blk - 1))]
        others.insert(n_blk - 2, others.pop(1))
        parts.append([part, *others])
    last, xs = [], {}
    kept = [{} for _ in range(CHUNKS)]
    late, owns = [], []

    def run(name, j, **how):
        wait = [v for key, i in WAITS.get((name, j), ()) for v in kept[i][key]]
        if j not in xs:
            xs[j] = join(f"join_{j}", parts[j], blk, list(last))
        value = products(f"{name}_{j}", tab, tiles, xs[j], wait=[*last, *wait], **how)
        last[:] = [value[-1]]
        return value

    def far(j, k):
        [a] = run("far", j, base=0, total=4, segs=[(0, 4, [], 0, 0)], ins=[], outs=[(4, True)])
        k["p1"] = send(a, pair)

    def ring1(j, k):
        h1, h2 = run(
            "ring1", j, base=16, total=4, ins=[k["p1"]], outs=[(2, True), (2, True)],
            segs=[(0, 2, [(0, 4, 0)], 0, 0), (2, 2, [(0, 4, 2)], 1, 0)],
        )
        k["r"] = send(h1, along(1, 0)), send(h2, along(-1, 0))

    def rest(j, k):
        [a] = run("rest", j, base=4, total=12, segs=[(0, 12, [], 0, 0)], ins=[], outs=[(12, True)])
        k["p2"] = [send(a, pair)]

    def ring2(j, k):
        m1, m2 = run(
            "ring2", j, base=20, total=8, ins=[*k["p2"], *k["r"]], outs=[(4, True), (4, True)],
            segs=[
                (0, 2, [(0, 12, 0), (1, 2, 0)], 0, 0),
                (2, 2, [(0, 12, 2)], 0, 2),
                (4, 2, [(0, 12, 4)], 1, 0),
                (6, 2, [(0, 12, 6), (2, 2, 0)], 1, 2),
            ],
        )
        k["n"] = send(m1, along(1, 0)), send(m2, along(-1, 0))

    def ring3(j, k):
        *t, own = run(
            "ring3", j, base=28, total=4, ins=[*k["p2"], *k["n"], *late], outs=[(1, True), (1, True), (1, True), (1, False)],
            segs=[(g, 1, [(0, 12, 8 + g), (1, 4, g), (2, 4, g)], g, 0) for g in range(4)], carry=len(late),
        )
        late[:] = t
        owns.append(own)

    for step, j in ORDER:
        dict(far=far, ring1=ring1, rest=rest, ring2=ring2, ring3=ring3)[step](j, kept[j])
    got = [send(t, along(k, 1)) for t, k in zip(late, (2, 1, -1))]
    return add_up(owns, got, last)


def solution(mesh):
    in_specs = (
        P(("blk", "dom"), None, None),
        P(("blk", "dom")),
        P(("blk", "dom")),
        P(("blk", "dom")),
        P(("blk", "dom"), None),
    )
    out_specs = P(("blk", "dom"), None)
    return jax.shard_map(shards, mesh=mesh, in_specs=in_specs, out_specs=out_specs, check_vma=False)
```

time: 110 us -> 108 us (0.982)
  local copies, waits for them, and re-layouts: 5.93 us -> 1.19 us
  waiting for transfers between devices: 39.6 us -> 43.4 us
  Pallas kernels: 34.2 us -> 36.9 us
  starting transfers between devices: 27.8 us -> 25.9 us
  other arithmetic: 1.38 us -> 0 us
    ppermute x6, waiting for transfers between devices: 2.25 us -> 10.2 us  [shards(): lax.ppermute(part, 'blk', ring(k))]
    unnamed x8 -> x4, local copies, waits for them, and re-layouts: 4.58 us -> 0.01 us
    ppermute x18 -> x15, waiting for transfers between devices: 37.3 us -> 33.2 us  [shards(): send = lambda value, pairs: lax.ppermute(value, 'dom', pairs)]
    pallas_call x12, Pallas kernels: 34 us -> 36.8 us  [the longest x10 30.2 us: products(): pl.pallas_call(functools.partial(kernel, base, total, segs, len(ins), len...]
    ppermute x18 -> x15, starting transfers between devices: 18 us -> 16.4 us  [shards(): send = lambda value, pairs: lax.ppermute(value, 'dom', pairs)]
    reduce_sum x6 -> x0, other arithmetic: 1.11 us -> none  [the longest x1 0.29 us: tables(): jnp.sum(jnp.where(t[:, None] == slot[None, :], xcol[None, :], 0), axis=1)]
  transfers between devices with their start and end apart: 24 -> 21, of which waited for: 10 -> 12; matrix products, arithmetic and copies ran while one was open for 1% -> 0% of each run, Pallas kernels for 30% -> 28%
where the time goes in v2:
time: 108 us
  waiting for transfers between devices  43.4 us (40%)
  Pallas kernels  36.9 us (34%)
  starting transfers between devices  25.9 us (24%)
  local copies, waits for them, and re-layouts  1.19 us (1%)
    ppermute x15, waiting for transfers between devices, shards(): send = lambda value, pairs: lax.ppermute(value, 'dom', pairs)  33.2 us
    pallas_call x10, Pallas kernels, products(): pl.pallas_call(functools.partial(kernel, base, total, segs, len(ins), len...  30.2 us
    ppermute x15, starting transfers between devices, shards(): send = lambda value, pairs: lax.ppermute(value, 'dom', pairs)  16.4 us
    ppermute x6, waiting for transfers between devices, shards(): lax.ppermute(part, 'blk', ring(k))  10.2 us
    ppermute x6, starting transfers between devices, shards(): lax.ppermute(part, 'blk', ring(k))  9.51 us
    pallas_call x1, Pallas kernels, prepare(): pl.pallas_call(functools.partial(prepare_kernel, pb, n_dom, n_blk), out_s...  5.13 us
  transfers between devices with their start and end apart: 21, of which 12 were waited for; matrix products, arithmetic and copies ran while one was open for 0% of the time, Pallas kernels for 28%

profile of v2, /device:TPU:14, one launch (start us, length us, event | category | flops | bytes accessed | tf_op | source)
XLA Modules:
  0.0 108.3 jit_solution(5750154361009205675)
XLA Ops:
  0.0 1.1 %fusion = (bf16[512,256]{1,0:T(8,128)(2,1)S(1)}, bf16[512,256]{1,0:T(8,128)(2,1)S(1)}) fusion(bf16[512,512]{1,0:T(8,128)(2,1)} %param.9), kind=kLoop, calls=%fused_computation | loop fusion | bytes 1048576 | tf_op jit(solution)/shard_map/slice | solution.py:263
  1.1 4.1 %collective-permute-start = (bf16[512,256]{1,0:T(8,128)(2,1)S(1)}, bf16[512,256]{1,0:T(8,128)(2,1)S(1)}, u32[]{:S(2)}, u32[]{:S(2)}) collective-permute-start(bf16[512,256]{1,0:T(8,128)(2,1)S(1)} %get-tuple-element.42), channel_id=1, source_target_pairs={{0,96},{32,0},{64,32},{96,64},{1,97},{33,1},{65,33},{97,65},{2,98}... | collective-permute-start | bytes 786440 | tf_op jit(solution)/shard_map/ppermute | solution.py:264
  5.2 1.3 %collective-permute-start.2 = (bf16[512,256]{1,0:T(8,128)(2,1)S(1)}, bf16[512,256]{1,0:T(8,128)(2,1)S(1)}, u32[]{:S(2)}, u32[]{:S(2)}) collective-permute-start(bf16[512,256]{1,0:T(8,128)(2,1)S(1)} %get-tuple-element.42), channel_id=1, source_target_pairs={{0,32},{32,64},{64,96},{96,0},{1,33},{33,65},{65,97},{97,1},{2,34}... | collective-permute-start | bytes 786440 | tf_op jit(solution)/shard_map/ppermute | solution.py:264
  7.2 0.1 stack.19.info
  7.3 5.1 %prepare.1 = (s32[8,384]{1,0:T(8,128)S(1)}, bf16[384,128,128]{2,1,0:T(8,128)(2,1)S(1)}) custom-call(s32[5]{0:T(128)S(1)} %stack.19.info, bf16[384,128,128]{2,1,0:T(8,128)(2,1)} %src.1, s32[1,384]{1,0:T(1,128)S(1)} %reshape.30.rows, s32[1,384]{1,0:T(1,128)S(1)} %reshape.31.cols), custom_call_target="tpu_custom_call" | custom-call | flops 4400000000 | bytes 1000 | tf_op jit(solution)/shard_map/prepare/pallas_call | solution.py:79
  12.4 4.0 %collective-permute-done = bf16[512,256]{1,0:T(8,128)(2,1)S(1)} collective-permute-done((bf16[512,256]{1,0:T(8,128)(2,1)S(1)}, bf16[512,256]{1,0:T(8,128)(2,1)S(1)}, u32[]{:S(2)}, u32[]{:S(2)}) %collective-permute-start) | collective-permute-done | bytes 262176 | tf_op jit(solution)/shard_map/ppermute | solution.py:264
  16.4 3.4 %collective-permute-done.2 = bf16[512,256]{1,0:T(8,128)(2,1)S(1)} collective-permute-done((bf16[512,256]{1,0:T(8,128)(2,1)S(1)}, bf16[512,256]{1,0:T(8,128)(2,1)S(1)}, u32[]{:S(2)}, u32[]{:S(2)}) %collective-permute-start.2) | collective-permute-done | bytes 262176 | tf_op jit(solution)/shard_map/ppermute | solution.py:264
  19.8 0.1 join_0.1.x
  19.9 2.0 %far_0.1.refs_1_ = s16[2064,256]{1,0:T(8,128)(2,1)S(1)} custom-call(s32[8,384]{1,0:T(8,128)S(1)} %get-tuple-element.23.tab, bf16[384,128,128]{2,1,0:T(8,128)(2,1)S(1)} %get-tuple-element.24.tiles, bf16[17,128,256]{2,1,0:T(8,128)(2,1)S(1)} %join_0.1.x), custom_call_target="tpu_custom_call" | custom-call | flops 17600000000 | bytes 1000 | tf_op jit(solution)/shard_map/far_0/pallas_call | solution.py:181
  21.9 0.1 collective-permute-start.3
  22.0 0.9 collective-permute-start.8
  22.9 1.3 %collective-permute-start.9 = (bf16[512,256]{1,0:T(8,128)(2,1)S(1)}, bf16[512,256]{1,0:T(8,128)(2,1)S(1)}, u32[]{:S(2)}, u32[]{:S(2)}) collective-permute-start(bf16[512,256]{1,0:T(8,128)(2,1)S(1)} %get-tuple-element.41), channel_id=1, source_target_pairs={{0,32},{32,64},{64,96},{96,0},{1,33},{33,65},{65,97},{97,1},{2,34}... | collective-permute-start | bytes 786440 | tf_op jit(solution)/shard_map/ppermute | solution.py:264
  24.1 2.0 %collective-permute-start.7 = (bf16[512,256]{1,0:T(8,128)(2,1)S(1)}, bf16[512,256]{1,0:T(8,128)(2,1)S(1)}, u32[]{:S(2)}, u32[]{:S(2)}) collective-permute-start(bf16[512,256]{1,0:T(8,128)(2,1)S(1)} %get-tuple-element.41), channel_id=1, source_target_pairs={{0,96},{32,0},{64,32},{96,64},{1,97},{33,1},{65,33},{97,65},{2,98}... | collective-permute-start | bytes 786440 | tf_op jit(solution)/shard_map/ppermute | solution.py:264
  26.1 2.1 %ring1_0.1 = (s16[1040,256]{1,0:T(8,128)(2,1)S(1)}, s16[1040,256]{1,0:T(8,128)(2,1)S(1)}) custom-call(s32[8,384]{1,0:T(8,128)S(1)} %get-tuple-element.23.tab, bf16[384,128,128]{2,1,0:T(8,128)(2,1)S(1)} %get-tuple-element.24.tiles, bf16[17,128,256]{2,1,0:T(8,128)(2,1)S(1)} %join_0.1.x, s16[2064,256]{1,0:T(8,128)(2,1)S(1)} %collective-permute-done.3.refs_0_, ...), custom_call_target="tpu_custom_call" | custom-call | flops 17600000000 | bytes 1000 | tf_op jit(solution)/shard_map/ring1_0/pallas_call | solution.py:181
  28.2 1.0 collective-permute-start.5
  29.2 1.1 %collective-permute-start.6 = (s16[1040,256]{1,0:T(8,128)(2,1)S(1)}, s16[1040,256]{1,0:T(8,128)(2,1)S(1)}, u32[]{:S(2)}, u32[]{:S(2)}) collective-permute-start(s16[1040,256]{1,0:T(8,128)(2,1)S(1)} %get-tuple-element.25.refs_0_), channel_id=1, source_target_pairs={{0,24},{1,7},{2,26},{3,1},{4,28},{5,3},{6,30},{7,5},{8,0},{9,15},{... | collective-permute-start | bytes 1597448 | tf_op jit(solution)/shard_map/ppermute | solution.py:258
  30.3 4.5 %rest_0.1.refs_4_.refs_0_ = s16[6160,256]{1,0:T(8,128)(2,1)S(1)} custom-call(s32[8,384]{1,0:T(8,128)S(1)} %get-tuple-element.23.tab, bf16[384,128,128]{2,1,0:T(8,128)(2,1)S(1)} %get-tuple-element.24.tiles, bf16[17,128,256]{2,1,0:T(8,128)(2,1)S(1)} %join_0.1.x, s16[1040,256]{1,0:T(8,128)(2,1)S(1)} %get-tuple-element.25.refs_0_), custom_call_target="tpu_custom_call" | custom-call | flops 52800000000 | bytes 1000 | tf_op jit(solution)/shard_map/rest_0/pallas_call | solution.py:181
  34.8 0.1 collective-permute-start.4
  34.9 2.8 %collective-permute-done.9 = bf16[512,256]{1,0:T(8,128)(2,1)S(1)} collective-permute-done((bf16[512,256]{1,0:T(8,128)(2,1)S(1)}, bf16[512,256]{1,0:T(8,128)(2,1)S(1)}, u32[]{:S(2)}, u32[]{:S(2)}) %collective-permute-start.9) | collective-permute-done | bytes 262176 | tf_op jit(solution)/shard_map/ppermute | solution.py:264
  37.7 0.1 join_1.1.x
  37.8 1.8 %collective-permute-done.6.refs_2_ = s16[1040,256]{1,0:T(8,128)(2,1)S(1)} collective-permute-done((s16[1040,256]{1,0:T(8,128)(2,1)S(1)}, s16[1040,256]{1,0:T(8,128)(2,1)S(1)}, u32[]{:S(2)}, u32[]{:S(2)}) %collective-permute-start.6) | collective-permute-done | bytes 532512 | tf_op jit(solution)/shard_map/ppermute | solution.py:258
  39.7 2.0 %far_1.1.refs_0_ = s16[2064,256]{1,0:T(8,128)(2,1)S(1)} custom-call(s32[8,384]{1,0:T(8,128)S(1)} %get-tuple-element.23.tab, bf16[384,128,128]{2,1,0:T(8,128)(2,1)S(1)} %get-tuple-element.24.tiles, bf16[17,128,256]{2,1,0:T(8,128)(2,1)S(1)} %join_1.1.x, s16[6160,256]{1,0:T(8,128)(2,1)S(1)} %rest_0.1.refs_4_.refs_0_, ...), custom_call_target="tpu_custom_call" | custom-call | flops 17600000000 | bytes 1000 | tf_op jit(solution)/shard_map/far_1/pallas_call | solution.py:181
  41.7 0.1 collective-permute-start.10
  41.8 4.5 %rest_1.1.refs_1_ = s16[6160,256]{1,0:T(8,128)(2,1)S(1)} custom-call(s32[8,384]{1,0:T(8,128)S(1)} %get-tuple-element.23.tab, bf16[384,128,128]{2,1,0:T(8,128)(2,1)S(1)} %get-tuple-element.24.tiles, bf16[17,128,256]{2,1,0:T(8,128)(2,1)S(1)} %join_1.1.x, s16[2064,256]{1,0:T(8,128)(2,1)S(1)} %far_1.1.refs_0_), custom_call_target="tpu_custom_call" | custom-call | flops 52800000000 | bytes 1000 | tf_op jit(solution)/shard_map/rest_1/pallas_call | solution.py:181
  46.2 1.6 %collective-permute-start.13 = (s16[6160,256]{1,0:T(8,128)(2,1)S(1)}, s16[6160,256]{1,0:T(8,128)(2,1)S(1)}, u32[]{:S(2)}, u32[]{:S(2)}) collective-permute-start(s16[6160,256]{1,0:T(8,128)(2,1)S(1)} %rest_1.1.refs_1_), channel_id=1, source_target_pairs={{0,1},{1,0},{2,3},{3,2},{4,5},{5,4},{6,7},{7,6},{8,9},{9,8},{10,11... | collective-permute-start | bytes 9461768 | tf_op jit(solution)/shard_map/ppermute | solution.py:258
  47.8 2.1 %ring1_1.1 = (s16[1040,256]{1,0:T(8,128)(2,1)S(1)}, s16[1040,256]{1,0:T(8,128)(2,1)S(1)}) custom-call(s32[8,384]{1,0:T(8,128)S(1)} %get-tuple-element.23.tab, bf16[384,128,128]{2,1,0:T(8,128)(2,1)S(1)} %get-tuple-element.24.tiles, bf16[17,128,256]{2,1,0:T(8,128)(2,1)S(1)} %join_1.1.x, s16[2064,256]{1,0:T(8,128)(2,1)S(1)} %collective-permute-done.10.refs_0_, ...), custom_call_target="tpu_custom_call" | custom-call | flops 17600000000 | bytes 1000 | tf_op jit(solution)/shard_map/ring1_1/pallas_call | solution.py:181
  49.9 0.1 collective-permute-start.14
  50.0 2.0 %collective-permute-start.15 = (s16[1040,256]{1,0:T(8,128)(2,1)S(1)}, s16[1040,256]{1,0:T(8,128)(2,1)S(1)}, u32[]{:S(2)}, u32[]{:S(2)}) collective-permute-start(s16[1040,256]{1,0:T(8,128)(2,1)S(1)} %get-tuple-element.27.refs_3_), channel_id=1, source_target_pairs={{0,24},{1,7},{2,26},{3,1},{4,28},{5,3},{6,30},{7,5},{8,0},{9,15},{... | collective-permute-start | bytes 1597448 | tf_op jit(solution)/shard_map/ppermute | solution.py:258
  52.0 3.7 %ring2_0.1 = (s16[2064,256]{1,0:T(8,128)(2,1)S(1)}, s16[2064,256]{1,0:T(8,128)(2,1)S(1)}) custom-call(s32[8,384]{1,0:T(8,128)S(1)} %get-tuple-element.23.tab, bf16[384,128,128]{2,1,0:T(8,128)(2,1)S(1)} %get-tuple-element.24.tiles, bf16[17,128,256]{2,1,0:T(8,128)(2,1)S(1)} %join_0.1.x, s16[6160,256]{1,0:T(8,128)(2,1)S(1)} %collective-permute-done.4.refs_0_, ...), custom_call_target="tpu_custom_call" | custom-call | flops 35200000000 | bytes 1000 | tf_op jit(solution)/shard_map/ring2_0/pallas_call | solution.py:181
  55.8 1.7 %collective-permute-start.11 = (s16[2064,256]{1,0:T(8,128)(2,1)S(1)}, s16[2064,256]{1,0:T(8,128)(2,1)S(1)}, u32[]{:S(2)}, u32[]{:S(2)}) collective-permute-start(s16[2064,256]{1,0:T(8,128)(2,1)S(1)} %get-tuple-element.28), channel_id=1, source_target_pairs={{0,8},{1,3},{2,10},{3,5},{4,12},{5,7},{6,14},{7,1},{8,16},{9,11},{... | collective-permute-start | bytes 3170312 | tf_op jit(solution)/shard_map/ppermute | solution.py:258
  57.5 0.4 collective-permute-start.12
  57.8 1.4 %collective-permute-done.14.refs_1_ = s16[1040,256]{1,0:T(8,128)(2,1)S(1)} collective-permute-done((s16[1040,256]{1,0:T(8,128)(2,1)S(1)}, s16[1040,256]{1,0:T(8,128)(2,1)S(1)}, u32[]{:S(2)}, u32[]{:S(2)}) %collective-permute-start.14) | collective-permute-done | bytes 532512 | tf_op jit(solution)/shard_map/ppermute | solution.py:258
  59.3 1.3 %collective-permute-done.15.refs_2_ = s16[1040,256]{1,0:T(8,128)(2,1)S(1)} collective-permute-done((s16[1040,256]{1,0:T(8,128)(2,1)S(1)}, s16[1040,256]{1,0:T(8,128)(2,1)S(1)}, u32[]{:S(2)}, u32[]{:S(2)}) %collective-permute-start.15) | collective-permute-done | bytes 532512 | tf_op jit(solution)/shard_map/ppermute | solution.py:258
  60.6 3.7 %ring2_1.1 = (s16[2064,256]{1,0:T(8,128)(2,1)S(1)}, s16[2064,256]{1,0:T(8,128)(2,1)S(1)}) custom-call(s32[8,384]{1,0:T(8,128)S(1)} %get-tuple-element.23.tab, bf16[384,128,128]{2,1,0:T(8,128)(2,1)S(1)} %get-tuple-element.24.tiles, bf16[17,128,256]{2,1,0:T(8,128)(2,1)S(1)} %join_1.1.x, s16[6160,256]{1,0:T(8,128)(2,1)S(1)} %collective-permute-done.13.refs_0_, ...), custom_call_target="tpu_custom_call" | custom-call | flops 35200000000 | bytes 1000 | tf_op jit(solution)/shard_map/ring2_1/pallas_call | solution.py:181
  64.3 1.3 %collective-permute-start.16 = (s16[2064,256]{1,0:T(8,128)(2,1)S(1)}, s16[2064,256]{1,0:T(8,128)(2,1)S(1)}, u32[]{:S(2)}, u32[]{:S(2)}) collective-permute-start(s16[2064,256]{1,0:T(8,128)(2,1)S(1)} %get-tuple-element.33), channel_id=1, source_target_pairs={{0,8},{1,3},{2,10},{3,5},{4,12},{5,7},{6,14},{7,1},{8,16},{9,11},{... | collective-permute-start | bytes 3170312 | tf_op jit(solution)/shard_map/ppermute | solution.py:258
  65.6 1.0 collective-permute-start.17
  66.6 4.1 %collective-permute-done.11.refs_1_ = s16[2064,256]{1,0:T(8,128)(2,1)S(1)} collective-permute-done((s16[2064,256]{1,0:T(8,128)(2,1)S(1)}, s16[2064,256]{1,0:T(8,128)(2,1)S(1)}, u32[]{:S(2)}, u32[]{:S(2)}) %collective-permute-start.11) | collective-permute-done | bytes 1056800 | tf_op jit(solution)/shard_map/ppermute | solution.py:258
  70.7 2.9 %collective-permute-done.12.refs_2_ = s16[2064,256]{1,0:T(8,128)(2,1)S(1)} collective-permute-done((s16[2064,256]{1,0:T(8,128)(2,1)S(1)}, s16[2064,256]{1,0:T(8,128)(2,1)S(1)}, u32[]{:S(2)}, u32[]{:S(2)}) %collective-permute-start.12) | collective-permute-done | bytes 1056800 | tf_op jit(solution)/shard_map/ppermute | solution.py:258
  73.6 2.8 %ring3_0.1 = (s16[528,256]{1,0:T(8,128)(2,1)S(1)}, s16[528,256]{1,0:T(8,128)(2,1)S(1)}, s16[528,256]{1,0:T(8,128)(2,1)S(1)}, f32[512,256]{1,0:T(8,128)S(1)}) custom-call(s32[8,384]{1,0:T(8,128)S(1)} %get-tuple-element.23.tab, bf16[384,128,128]{2,1,0:T(8,128)(2,1)S(1)} %get-tuple-element.24.tiles, bf16[17,128,256]{2,1,0:T(8,128)(2,1)S(1)} %join_0.1.x, ...), custom_call_target="tpu_custom_call" | custom-call | flops 17600000000 | bytes 1000 | tf_op jit(solution)/shard_map/ring3_0/pallas_call | solution.py:181
  76.4 5.6 %collective-permute-done.16.refs_1_ = s16[2064,256]{1,0:T(8,128)(2,1)S(1)} collective-permute-done((s16[2064,256]{1,0:T(8,128)(2,1)S(1)}, s16[2064,256]{1,0:T(8,128)(2,1)S(1)}, u32[]{:S(2)}, u32[]{:S(2)}) %collective-permute-start.16) | collective-permute-done | bytes 1056800 | tf_op jit(solution)/shard_map/ppermute | solution.py:258
  82.0 2.9 %collective-permute-done.17.refs_2_ = s16[2064,256]{1,0:T(8,128)(2,1)S(1)} collective-permute-done((s16[2064,256]{1,0:T(8,128)(2,1)S(1)}, s16[2064,256]{1,0:T(8,128)(2,1)S(1)}, u32[]{:S(2)}, u32[]{:S(2)}) %collective-permute-start.17) | collective-permute-done | bytes 1056800 | tf_op jit(solution)/shard_map/ppermute | solution.py:258
  84.9 2.9 %ring3_1.1 = (s16[1056,256]{1,0:T(8,128)(2,1)S(1)}, s16[1056,256]{1,0:T(8,128)(2,1)S(1)}, s16[1056,256]{1,0:T(8,128)(2,1)S(1)}, f32[512,256]{1,0:T(8,128)S(1)}) custom-call(s32[8,384]{1,0:T(8,128)S(1)} %get-tuple-element.23.tab, bf16[384,128,128]{2,1,0:T(8,128)(2,1)S(1)} %get-tuple-element.24.tiles, bf16[17,128,256]{2,1,0:T(8,128)(2,1)S(1)} %join_1.1.x, ...), custom_call_target="tpu_custom_call" | custom-call | flops 17600000000 | bytes 1000 | tf_op jit(solution)/shard_map/ring3_1/pallas_call | solution.py:181
  87.7 0.1 collective-permute-start.18
  87.8 3.9 %collective-permute-start.19 = (s16[1056,256]{1,0:T(8,128)(2,1)S(1)}, s16[1056,256]{1,0:T(8,128)(2,1)S(1)}, u32[]{:S(2)}, u32[]{:S(2)}) collective-permute-start(s16[1056,256]{1,0:T(8,128)(2,1)S(1)} %get-tuple-element.39), channel_id=1, source_target_pairs={{0,2},{1,9},{2,4},{3,11},{4,6},{5,13},{6,0},{7,15},{8,10},{9,17},{... | collective-permute-start | bytes 1622024 | tf_op jit(solution)/shard_map/ppermute | solution.py:258
  91.7 2.0 %collective-permute-start.20 = (s16[1056,256]{1,0:T(8,128)(2,1)S(1)}, s16[1056,256]{1,0:T(8,128)(2,1)S(1)}, u32[]{:S(2)}, u32[]{:S(2)}) collective-permute-start(s16[1056,256]{1,0:T(8,128)(2,1)S(1)} %get-tuple-element.40), channel_id=1, source_target_pairs={{0,6},{1,25},{2,0},{3,27},{4,2},{5,29},{6,4},{7,31},{8,14},{9,1},{... | collective-permute-start | bytes 1622024 | tf_op jit(solution)/shard_map/ppermute | solution.py:258
  93.7 5.1 %collective-permute-done.18.refs_2_ = s16[1056,256]{1,0:T(8,128)(2,1)S(1)} collective-permute-done((s16[1056,256]{1,0:T(8,128)(2,1)S(1)}, s16[1056,256]{1,0:T(8,128)(2,1)S(1)}, u32[]{:S(2)}, u32[]{:S(2)}) %collective-permute-start.18) | collective-permute-done | bytes 540704 | tf_op jit(solution)/shard_map/ppermute | solution.py:258
  98.8 8.1 %collective-permute-done.19.refs_3_ = s16[1056,256]{1,0:T(8,128)(2,1)S(1)} collective-permute-done((s16[1056,256]{1,0:T(8,128)(2,1)S(1)}, s16[1056,256]{1,0:T(8,128)(2,1)S(1)}, u32[]{:S(2)}, u32[]{:S(2)}) %collective-permute-start.19) | collective-permute-done | bytes 540704 | tf_op jit(solution)/shard_map/ppermute | solution.py:258
  106.9 1.4 %add_up.1 = f32[512,512]{1,0:T(8,128)} custom-call(f32[512,256]{1,0:T(8,128)S(1)} %get-tuple-element.32.refs_6_.refs_0_, f32[512,256]{1,0:T(8,128)S(1)} %get-tuple-element.37.refs_1_.refs_5_, s16[1056,256]{1,0:T(8,128)(2,1)S(1)} %collective-permute-done.18.refs_2_, s16[1056,256]{1,0:T(8,128)(2,1)S(1)} %collective-permute-done.19.refs_3_, ...), custom_call_target="tpu_custom_call" | custom-call | tf_op jit(solution)/shard_map/add_up/pallas_call | solution.py:235
  (16 shorter events, 0.0 us)
Async XLA Ops:
  0.0 7.1 %copy-start = (s32[384]{0:T(512)S(1)}, s32[384]{0:T(512)}, u32[]{:S(2)}) copy-start(s32[384]{0:T(512)} %param.6) | copy-start | bytes 4612
  0.0 7.1 %copy-start.1 = (s32[384]{0:T(512)S(1)}, s32[384]{0:T(512)}, u32[]{:S(2)}) copy-start(s32[384]{0:T(512)} %param.7) | copy-start | bytes 4612
  1.1 15.3 %collective-permute-start = (bf16[512,256]{1,0:T(8,128)(2,1)S(1)}, bf16[512,256]{1,0:T(8,128)(2,1)S(1)}, u32[]{:S(2)}, u32[]{:S(2)}) collective-permute-start(bf16[512,256]{1,0:T(8,128)(2,1)S(1)} %get-tuple-element.42), channel_id=1, source_target_pairs={{0,96},{32,0},{64,32},{96,64},{1,97},{33,1},{65,33},{97,65},{2,98}... | collective-permute-start | bytes 786440 | tf_op jit(solution)/shard_map/ppermute | solution.py:264
  5.2 11.2 %collective-permute-start.1 = (bf16[512,256]{1,0:T(8,128)(2,1)S(1)}, bf16[512,256]{1,0:T(8,128)(2,1)S(1)}, u32[]{:S(2)}, u32[]{:S(2)}) collective-permute-start(bf16[512,256]{1,0:T(8,128)(2,1)S(1)} %get-tuple-element.42), channel_id=1, source_target_pairs={{0,64},{32,96},{64,0},{96,32},{1,65},{33,97},{65,1},{97,33},{2,66}... | collective-permute-start | bytes 786440 | tf_op jit(solution)/shard_map/ppermute | solution.py:264
  5.2 14.6 %collective-permute-start.2 = (bf16[512,256]{1,0:T(8,128)(2,1)S(1)}, bf16[512,256]{1,0:T(8,128)(2,1)S(1)}, u32[]{:S(2)}, u32[]{:S(2)}) collective-permute-start(bf16[512,256]{1,0:T(8,128)(2,1)S(1)} %get-tuple-element.42), channel_id=1, source_target_pairs={{0,32},{32,64},{64,96},{96,0},{1,33},{33,65},{65,97},{97,1},{2,34}... | collective-permute-start | bytes 786440 | tf_op jit(solution)/shard_map/ppermute | solution.py:264
  21.9 4.2 %collective-permute-start.3 = (s16[2064,256]{1,0:T(8,128)(2,1)S(1)}, s16[2064,256]{1,0:T(8,128)(2,1)S(1)}, u32[]{:S(2)}, u32[]{:S(2)}) collective-permute-start(s16[2064,256]{1,0:T(8,128)(2,1)S(1)} %far_0.1.refs_1_), channel_id=1, source_target_pairs={{0,1},{1,0},{2,3},{3,2},{4,5},{5,4},{6,7},{7,6},{8,9},{9,8},{10,11... | collective-permute-start | bytes 3170312 | tf_op jit(solution)/shard_map/ppermute | solution.py:258
  22.0 12.8 %collective-permute-start.8 = (bf16[512,256]{1,0:T(8,128)(2,1)S(1)}, bf16[512,256]{1,0:T(8,128)(2,1)S(1)}, u32[]{:S(2)}, u32[]{:S(2)}) collective-permute-start(bf16[512,256]{1,0:T(8,128)(2,1)S(1)} %get-tuple-element.41), channel_id=1, source_target_pairs={{0,64},{32,96},{64,0},{96,32},{1,65},{33,97},{65,1},{97,33},{2,66}... | collective-permute-start | bytes 786440 | tf_op jit(solution)/shard_map/ppermute | solution.py:264
  22.9 14.9 %collective-permute-start.9 = (bf16[512,256]{1,0:T(8,128)(2,1)S(1)}, bf16[512,256]{1,0:T(8,128)(2,1)S(1)}, u32[]{:S(2)}, u32[]{:S(2)}) collective-permute-start(bf16[512,256]{1,0:T(8,128)(2,1)S(1)} %get-tuple-element.41), channel_id=1, source_target_pairs={{0,32},{32,64},{64,96},{96,0},{1,33},{33,65},{65,97},{97,1},{2,34}... | collective-permute-start | bytes 786440 | tf_op jit(solution)/shard_map/ppermute | solution.py:264
  24.1 13.6 %collective-permute-start.7 = (bf16[512,256]{1,0:T(8,128)(2,1)S(1)}, bf16[512,256]{1,0:T(8,128)(2,1)S(1)}, u32[]{:S(2)}, u32[]{:S(2)}) collective-permute-start(bf16[512,256]{1,0:T(8,128)(2,1)S(1)} %get-tuple-element.41), channel_id=1, source_target_pairs={{0,96},{32,0},{64,32},{96,64},{1,97},{33,1},{65,33},{97,65},{2,98}... | collective-permute-start | bytes 786440 | tf_op jit(solution)/shard_map/ppermute | solution.py:264
  28.2 9.6 %collective-permute-start.5 = (s16[1040,256]{1,0:T(8,128)(2,1)S(1)}, s16[1040,256]{1,0:T(8,128)(2,1)S(1)}, u32[]{:S(2)}, u32[]{:S(2)}) collective-permute-start(s16[1040,256]{1,0:T(8,128)(2,1)S(1)} %get-tuple-element.26), channel_id=1, source_target_pairs={{0,8},{1,3},{2,10},{3,5},{4,12},{5,7},{6,14},{7,1},{8,16},{9,11},{... | collective-permute-start | bytes 1597448 | tf_op jit(solution)/shard_map/ppermute | solution.py:258
  29.2 10.5 %collective-permute-start.6 = (s16[1040,256]{1,0:T(8,128)(2,1)S(1)}, s16[1040,256]{1,0:T(8,128)(2,1)S(1)}, u32[]{:S(2)}, u32[]{:S(2)}) collective-permute-start(s16[1040,256]{1,0:T(8,128)(2,1)S(1)} %get-tuple-element.25.refs_0_), channel_id=1, source_target_pairs={{0,24},{1,7},{2,26},{3,1},{4,28},{5,3},{6,30},{7,5},{8,0},{9,15},{... | collective-permute-start | bytes 1597448 | tf_op jit(solution)/shard_map/ppermute | solution.py:258
  34.8 17.2 %collective-permute-start.4 = (s16[6160,256]{1,0:T(8,128)(2,1)S(1)}, s16[6160,256]{1,0:T(8,128)(2,1)S(1)}, u32[]{:S(2)}, u32[]{:S(2)}) collective-permute-start(s16[6160,256]{1,0:T(8,128)(2,1)S(1)} %rest_0.1.refs_4_.refs_0_), channel_id=1, source_target_pairs={{0,1},{1,0},{2,3},{3,2},{4,5},{5,4},{6,7},{7,6},{8,9},{9,8},{10,11... | collective-permute-start | bytes 9461768 | tf_op jit(solution)/shard_map/ppermute | solution.py:258
  41.7 6.2 %collective-permute-start.10 = (s16[2064,256]{1,0:T(8,128)(2,1)S(1)}, s16[2064,256]{1,0:T(8,128)(2,1)S(1)}, u32[]{:S(2)}, u32[]{:S(2)}) collective-permute-start(s16[2064,256]{1,0:T(8,128)(2,1)S(1)} %far_1.1.refs_0_), channel_id=1, source_target_pairs={{0,1},{1,0},{2,3},{3,2},{4,5},{5,4},{6,7},{7,6},{8,9},{9,8},{10,11... | collective-permute-start | bytes 3170312 | tf_op jit(solution)/shard_map/ppermute | solution.py:258
  46.2 14.3 %collective-permute-start.13 = (s16[6160,256]{1,0:T(8,128)(2,1)S(1)}, s16[6160,256]{1,0:T(8,128)(2,1)S(1)}, u32[]{:S(2)}, u32[]{:S(2)}) collective-permute-start(s16[6160,256]{1,0:T(8,128)(2,1)S(1)} %rest_1.1.refs_1_), channel_id=1, source_target_pairs={{0,1},{1,0},{2,3},{3,2},{4,5},{5,4},{6,7},{7,6},{8,9},{9,8},{10,11... | collective-permute-start | bytes 9461768 | tf_op jit(solution)/shard_map/ppermute | solution.py:258
  49.9 9.3 %collective-permute-start.14 = (s16[1040,256]{1,0:T(8,128)(2,1)S(1)}, s16[1040,256]{1,0:T(8,128)(2,1)S(1)}, u32[]{:S(2)}, u32[]{:S(2)}) collective-permute-start(s16[1040,256]{1,0:T(8,128)(2,1)S(1)} %get-tuple-element.30), channel_id=1, source_target_pairs={{0,8},{1,3},{2,10},{3,5},{4,12},{5,7},{6,14},{7,1},{8,16},{9,11},{... | collective-permute-start | bytes 1597448 | tf_op jit(solution)/shard_map/ppermute | solution.py:258
  50.0 10.5 %collective-permute-start.15 = (s16[1040,256]{1,0:T(8,128)(2,1)S(1)}, s16[1040,256]{1,0:T(8,128)(2,1)S(1)}, u32[]{:S(2)}, u32[]{:S(2)}) collective-permute-start(s16[1040,256]{1,0:T(8,128)(2,1)S(1)} %get-tuple-element.27.refs_3_), channel_id=1, source_target_pairs={{0,24},{1,7},{2,26},{3,1},{4,28},{5,3},{6,30},{7,5},{8,0},{9,15},{... | collective-permute-start | bytes 1597448 | tf_op jit(solution)/shard_map/ppermute | solution.py:258
  55.8 15.0 %collective-permute-start.11 = (s16[2064,256]{1,0:T(8,128)(2,1)S(1)}, s16[2064,256]{1,0:T(8,128)(2,1)S(1)}, u32[]{:S(2)}, u32[]{:S(2)}) collective-permute-start(s16[2064,256]{1,0:T(8,128)(2,1)S(1)} %get-tuple-element.28), channel_id=1, source_target_pairs={{0,8},{1,3},{2,10},{3,5},{4,12},{5,7},{6,14},{7,1},{8,16},{9,11},{... | collective-permute-start | bytes 3170312 | tf_op jit(solution)/shard_map/ppermute | solution.py:258
  57.5 16.1 %collective-permute-start.12 = (s16[2064,256]{1,0:T(8,128)(2,1)S(1)}, s16[2064,256]{1,0:T(8,128)(2,1)S(1)}, u32[]{:S(2)}, u32[]{:S(2)}) collective-permute-start(s16[2064,256]{1,0:T(8,128)(2,1)S(1)} %get-tuple-element.29.refs_3_), channel_id=1, source_target_pairs={{0,24},{1,7},{2,26},{3,1},{4,28},{5,3},{6,30},{7,5},{8,0},{9,15},{... | collective-permute-start | bytes 3170312 | tf_op jit(solution)/shard_map/ppermute | solution.py:258
  64.3 17.7 %collective-permute-start.16 = (s16[2064,256]{1,0:T(8,128)(2,1)S(1)}, s16[2064,256]{1,0:T(8,128)(2,1)S(1)}, u32[]{:S(2)}, u32[]{:S(2)}) collective-permute-start(s16[2064,256]{1,0:T(8,128)(2,1)S(1)} %get-tuple-element.33), channel_id=1, source_target_pairs={{0,8},{1,3},{2,10},{3,5},{4,12},{5,7},{6,14},{7,1},{8,16},{9,11},{... | collective-permute-start | bytes 3170312 | tf_op jit(solution)/shard_map/ppermute | solution.py:258
  65.6 19.3 %collective-permute-start.17 = (s16[2064,256]{1,0:T(8,128)(2,1)S(1)}, s16[2064,256]{1,0:T(8,128)(2,1)S(1)}, u32[]{:S(2)}, u32[]{:S(2)}) collective-permute-start(s16[2064,256]{1,0:T(8,128)(2,1)S(1)} %get-tuple-element.31.refs_3_), channel_id=1, source_target_pairs={{0,24},{1,7},{2,26},{3,1},{4,28},{5,3},{6,30},{7,5},{8,0},{9,15},{... | collective-permute-start | bytes 3170312 | tf_op jit(solution)/shard_map/ppermute | solution.py:258
  87.7 11.0 %collective-permute-start.18 = (s16[1056,256]{1,0:T(8,128)(2,1)S(1)}, s16[1056,256]{1,0:T(8,128)(2,1)S(1)}, u32[]{:S(2)}, u32[]{:S(2)}) collective-permute-start(s16[1056,256]{1,0:T(8,128)(2,1)S(1)} %get-tuple-element.38), channel_id=1, source_target_pairs={{0,4},{1,17},{2,6},{3,19},{4,0},{5,21},{6,2},{7,23},{8,12},{9,25},... | collective-permute-start | bytes 1622024 | tf_op jit(solution)/shard_map/ppermute | solution.py:258
  87.8 19.0 %collective-permute-start.19 = (s16[1056,256]{1,0:T(8,128)(2,1)S(1)}, s16[1056,256]{1,0:T(8,128)(2,1)S(1)}, u32[]{:S(2)}, u32[]{:S(2)}) collective-permute-start(s16[1056,256]{1,0:T(8,128)(2,1)S(1)} %get-tuple-element.39), channel_id=1, source_target_pairs={{0,2},{1,9},{2,4},{3,11},{4,6},{5,13},{6,0},{7,15},{8,10},{9,17},{... | collective-permute-start | bytes 1622024 | tf_op jit(solution)/shard_map/ppermute | solution.py:258
  91.7 15.2 %collective-permute-start.20 = (s16[1056,256]{1,0:T(8,128)(2,1)S(1)}, s16[1056,256]{1,0:T(8,128)(2,1)S(1)}, u32[]{:S(2)}, u32[]{:S(2)}) collective-permute-start(s16[1056,256]{1,0:T(8,128)(2,1)S(1)} %get-tuple-element.40), channel_id=1, source_target_pairs={{0,6},{1,25},{2,0},{3,27},{4,2},{5,29},{6,4},{7,31},{8,14},{9,1},{... | collective-permute-start | bytes 1622024 | tf_op jit(solution)/shard_map/ppermute | solution.py:258
